TPU v7x, 256 devices: a whole 4x4x8 slice. The times are simulated.
256 devices in a mesh: gx: 32 (over y_lo, z, core), gy: 8 (over x, y_hi).
Axes of the slice: x: 4, y: 4 (y_hi: 2, y_lo: 2; y = y_hi * 2 + y_lo), z: 8, core: 2. Of those that a mesh axis runs over, the one named last changes fastest.
Arguments:
- features: bfloat16 [32, 8, 128, 128], P('gx', 'gy'), may hold values from -6 to 6
- positions: float32 [32, 8, 3, 128], P('gx', 'gy'), may hold values from 0 to 4
- neighbours: int32 [32, 8, 32, 128], P('gx', 'gy'), may hold values from 0 to 287, as said below
- neighbour_counts: int32 [32, 8, 128], P('gx', 'gy'), may hold values from 16 to 32, as said below
- domain_counts: int32 [32, 8], P('gx', 'gy'), may hold values from 64 to 128, as said below
- face_lists: int32 [32, 8, 2, 64], P('gx', 'gy'), may hold values from 0 to 127, as said below
- corner_lists: int32 [32, 8, 2, 16], P('gx', 'gy'), may hold values from 0 to 127, as said below
- w_center: bfloat16 [128, 128], replicated, may hold values from -0.5 to 0.5
- w_neigh: bfloat16 [128, 128], replicated, may hold values from -0.5 to 0.5
- w_radial: float32 [8, 128], replicated, may hold values from -2 to 2
- w_latent: bfloat16 [128, 128], replicated, may hold values from -0.5 to 0.5
- w_readout: bfloat16 [384, 128], replicated, may hold values from -0.3125 to 0.3125
- w_energy: float32 [128], replicated, may hold values from -0.5 to 0.5
Outputs:
- energy: float32 [], replicated
- forces: float32 [32, 8, 3, 128], P('gx', 'gy')
Inputs may be any that keep to these rules, and one draw needn't show every extreme that they name: `domain_counts`: each domain's count is at least half its slots, and some domain is full. `neighbour_counts`: some atom of every domain uses all slots. `neighbours`: an index is a live own atom (below the domain's count) or a ghost slot (128 to 287), never the atom itself. `face_lists`: every index is a live atom of the sending domain; an atom may appear more than once. `corner_lists`: every index is a live atom of the sending domain; an atom may appear more than once.
All inputs are finite; a program needn't handle non-finite values.
Results may differ from a plain program's by a relative error of at most 0.011.
Values sent between devices are 32-bit elements; how exact they have to be, the bound alone decides.
A program may use at most 128 MiB of HBM per device.

v0:
```python
import math

import jax
import jax.numpy as jnp
from jax import lax
from jax.sharding import PartitionSpec as P

cutoff = 6.0
soften = 0.25
box_width = 4.0
parity = (1.0, -1.0, -1.0, -1.0, 1.0, 1.0, 1.0, 1.0, 1.0)


def from_behind(block, axis, distance):
    devices = range(lax.axis_size(axis))
    route = [((i - distance) % len(devices), i) for i in devices]
    return lax.ppermute(block, axis, route)


def harmonics(unit):
    along_x, along_y, along_z = (unit[0], unit[1], unit[2])
    root3 = math.sqrt(3.0)
    root15 = math.sqrt(15.0)
    root5 = math.sqrt(5.0)
    return jnp.stack(
        [
            jnp.ones_like(along_x),
            root3 * along_x,
            root3 * along_y,
            root3 * along_z,
            root15 * along_x * along_y,
            root15 * along_y * along_z,
            0.5 * root5 * (3.0 * along_z * along_z - 1.0),
            root15 * along_x * along_z,
            0.5 * root15 * (along_x * along_x - along_y * along_y),
        ]
    )


def pair_terms(placed, neigh_all, center_proj, nbr_index, pair_live, w_radial, w_latent):
    n_atoms = center_proj.shape[0]
    total_rows = neigh_all.shape[0]
    slots = nbr_index.shape[0]
    width = center_proj.shape[1]
    anchor = placed[:, :n_atoms]
    other = jnp.take(placed, nbr_index, axis=1)
    delta = other - anchor[:, None, :]
    radius = jnp.sqrt(jnp.sum(delta * delta, axis=0) + soften)
    unit = delta / radius[None]
    scaled = jnp.minimum(radius / cutoff, 1.0)
    envelope = 1.0 - 28.0 * scaled**6 + 48.0 * scaled**7 - 21.0 * scaled**8
    orders = jnp.arange(1, w_radial.shape[0] + 1).astype(jnp.float32)
    basis = (
        math.sqrt(2.0 / cutoff)
        * jnp.sin(orders[:, None, None] * (math.pi / cutoff) * radius[None])
        / radius[None]
    )
    radial = jnp.einsum("nka,nc->kac", basis, w_radial, precision=lax.Precision.HIGHEST)
    pre_act = center_proj[None] + jnp.take(neigh_all, nbr_index, axis=0) + radial
    hidden = jax.nn.silu(pre_act).astype(jnp.bfloat16)
    latent = jax.nn.silu(
        jnp.dot(
            hidden.reshape(slots * n_atoms, width), w_latent, preferred_element_type=jnp.float32
        )
    ).reshape(slots, n_atoms, width)
    weight = latent * (envelope * pair_live)[:, :, None]
    harm = harmonics(unit)
    center_sum = jnp.einsum("mka,kac->amc", harm, weight, precision=lax.Precision.HIGHEST).reshape(
        n_atoms, 9 * width
    )
    block = math.gcd(slots, 8)
    groups = slots // block
    signs = jnp.array(parity, dtype=jnp.float32)
    signed = jnp.transpose(
        (harm * signs[:, None, None]).reshape(9, groups, block * n_atoms), (1, 0, 2)
    )
    weight_blocks = weight.reshape(groups, block * n_atoms, width)
    index_blocks = nbr_index.reshape(groups, block * n_atoms)

    def add_block(carry, item):
        harm_block, weight_block, index_block = item
        term = (jnp.transpose(harm_block)[:, :, None] * weight_block[:, None, :]).reshape(
            -1, 9 * width
        )
        return (carry + jax.ops.segment_sum(term, index_block, num_segments=total_rows), None)

    start = jnp.zeros((total_rows, 9 * width), dtype=weight.dtype)
    scattered, unused = lax.scan(add_block, start, (signed, weight_blocks, index_blocks))
    return scattered.at[:n_atoms, :].add(center_sum)


def readout(moments, atom_live, w_readout, w_energy):
    n_atoms = moments.shape[0]
    shaped = moments.reshape(n_atoms, 9, -1)
    squares = shaped * shaped
    invariants = jnp.stack(
        [
            jnp.log1p(squares[:, 0]),
            jnp.log1p(jnp.sum(squares[:, 1:4], axis=1)),
            jnp.log1p(jnp.sum(squares[:, 4:9], axis=1)),
        ],
        axis=1,
    )
    packed = invariants.reshape(n_atoms, -1).astype(jnp.bfloat16)
    hidden = jax.nn.silu(jnp.dot(packed, w_readout, preferred_element_type=jnp.float32))
    energies = jnp.dot(hidden, w_energy, precision=lax.Precision.HIGHEST)
    return jnp.sum(energies * atom_live)


def send_features(neigh_proj, own_pos, faces, corners):
    face_rows = faces.shape[1]
    corner_rows = corners.shape[1]
    first_rows = jnp.concatenate([faces[0], corners[0], corners[1]])
    proj_first, pos_first = from_behind(
        (jnp.take(neigh_proj, first_rows, axis=0), jnp.take(own_pos, first_rows, axis=1)), "gx", -1
    )
    upper_end = face_rows + corner_rows
    proj_second, pos_second = from_behind(
        (
            jnp.concatenate(
                [jnp.take(neigh_proj, faces[1], axis=0), proj_first[face_rows:upper_end]], axis=0
            ),
            jnp.concatenate(
                [jnp.take(own_pos, faces[1], axis=1), pos_first[:, face_rows:upper_end]], axis=1
            ),
        ),
        "gy",
        -1,
    )
    proj_third, pos_third = from_behind((proj_first[upper_end:], pos_first[:, upper_end:]), "gy", 1)
    ghost_proj = jnp.concatenate([proj_first[:face_rows], proj_second, proj_third], axis=0)
    shift_x = jnp.concatenate(
        [
            jnp.full((face_rows,), box_width),
            jnp.zeros((face_rows,)),
            jnp.full((2 * corner_rows,), box_width),
        ]
    )
    shift_y = jnp.concatenate(
        [
            jnp.zeros((face_rows,)),
            jnp.full((face_rows,), box_width),
            jnp.full((corner_rows,), box_width),
            jnp.full((corner_rows,), -box_width),
        ]
    )
    offsets = jnp.stack([shift_x, shift_y, jnp.zeros_like(shift_x)])
    ghost_pos = jnp.concatenate([pos_first[:, :face_rows], pos_second, pos_third], axis=1) + offsets
    return (ghost_proj, ghost_pos)


def return_sums(ghost_moments, face_rows, corner_rows):
    upper_end = 2 * face_rows + corner_rows
    face_x = ghost_moments[:face_rows]
    face_y = ghost_moments[face_rows : 2 * face_rows]
    upper = ghost_moments[2 * face_rows : upper_end]
    lower = ghost_moments[upper_end:]
    back_x = from_behind(face_x, "gx", 1)
    back_y = from_behind(face_y, "gy", 1)
    back_up = from_behind(from_behind(upper, "gy", 1), "gx", 1)
    back_down = from_behind(from_behind(lower, "gy", -1), "gx", 1)
    return jnp.concatenate([back_x, back_y, back_up, back_down], axis=0)


def send_slopes(slope, faces, corners):
    slope_x = from_behind(jnp.take(slope, faces[0], axis=0), "gx", -1)
    slope_y = from_behind(jnp.take(slope, faces[1], axis=0), "gy", -1)
    slope_up = from_behind(from_behind(jnp.take(slope, corners[0], axis=0), "gx", -1), "gy", -1)
    slope_down = from_behind(from_behind(jnp.take(slope, corners[1], axis=0), "gx", -1), "gy", 1)
    return jnp.concatenate([slope_x, slope_y, slope_up, slope_down], axis=0)


def return_forces(ghost_grads, face_rows, corner_rows):
    upper_end = 2 * face_rows + corner_rows
    face_x = ghost_grads[:, :face_rows]
    along_y = from_behind(ghost_grads[:, face_rows:upper_end], "gy", 1)
    middle = from_behind(ghost_grads[:, upper_end:], "gy", -1)
    along_x = from_behind(
        jnp.concatenate([face_x, along_y[:, face_rows:], middle], axis=1), "gx", 1
    )
    return jnp.concatenate(
        [along_x[:, :face_rows], along_y[:, :face_rows], along_x[:, face_rows:]], axis=1
    )


def on_device(
    features,
    positions,
    neighbours,
    neighbour_counts,
    domain_counts,
    face_lists,
    corner_lists,
    w_center,
    w_neigh,
    w_radial,
    w_latent,
    w_readout,
    w_energy,
):
    atom_feat = features[0, 0]
    own_pos = positions[0, 0]
    nbr_index = neighbours[0, 0]
    slot_counts = neighbour_counts[0, 0]
    live_count = domain_counts[0, 0]
    faces = face_lists[0, 0]
    corners = corner_lists[0, 0]
    n_atoms = atom_feat.shape[0]
    slots = nbr_index.shape[0]
    face_rows = faces.shape[1]
    corner_rows = corners.shape[1]
    atom_flag = jnp.arange(n_atoms) < live_count
    atom_live = atom_flag.astype(jnp.float32)
    pair_live = ((jnp.arange(slots)[:, None] < slot_counts[None, :]) & atom_flag[None, :]).astype(
        jnp.float32
    )
    center_proj = jnp.dot(atom_feat, w_center, preferred_element_type=jnp.float32)
    neigh_proj = jnp.dot(atom_feat, w_neigh, preferred_element_type=jnp.float32)
    ghost_proj, ghost_pos = send_features(neigh_proj, own_pos, faces, corners)
    all_pos = jnp.concatenate([own_pos, ghost_pos], axis=1)
    all_proj = jnp.concatenate([neigh_proj, ghost_proj], axis=0)
    moments, pull_pairs = jax.vjp(
        lambda placed: pair_terms(
            placed, all_proj, center_proj, nbr_index, pair_live, w_radial, w_latent
        ),
        all_pos,
    )
    send_rows = jnp.concatenate([faces[0], faces[1], corners[0], corners[1]])
    returned = return_sums(moments[n_atoms:], face_rows, corner_rows)
    own_moments = moments[:n_atoms].at[send_rows].add(returned)
    local_total, pull_read = jax.vjp(
        lambda values: readout(values, atom_live, w_readout, w_energy), own_moments
    )
    slope = pull_read(jnp.ones((), jnp.float32))[0]
    summed = lax.psum((local_total, live_count.astype(jnp.float32)), ("gx", "gy"))
    energy = summed[0] / summed[1]
    ghost_slope = send_slopes(slope, faces, corners)
    grads = pull_pairs(jnp.concatenate([slope, ghost_slope], axis=0))[0]
    back_grads = return_forces(grads[:, n_atoms:], face_rows, corner_rows)
    own_grads = grads[:, :n_atoms].at[:, send_rows].add(back_grads)
    return (energy, (-own_grads)[None, None])


def solution(mesh):
    placed = (
        P("gx", "gy", None, None),
        P("gx", "gy", None, None),
        P("gx", "gy", None, None),
        P("gx", "gy", None),
        P("gx", "gy"),
        P("gx", "gy", None, None),
        P("gx", "gy", None, None),
        P(),
        P(),
        P(),
        P(),
        P(),
        P(),
    )
    return jax.shard_map(
        on_device,
        mesh=mesh,
        in_specs=placed,
        out_specs=(P(), P("gx", "gy", None, None)),
        check_vma=False,
    )
```

profile of v0, /device:TPU:1, one launch (start us, length us, event | category | flops | bytes accessed | tf_op | source)
XLA Modules:
  0.0 492.3 jit_solution(4639364930889732430)
XLA Ops:
  9.4 4.6 collective-permute-start.3
  25.6 4.9 collective-permute-start.1
  32.5 6.1 %collective-permute-done.2 = f32[3,16]{0,1:T(8,128)S(1)} collective-permute-done((f32[3,16]{0,1:T(8,128)S(1)}, f32[3,16]{0,1:T(8,128)S(1)}, u32[]{:S(2)}, u32[]{:S(2)}) %collective-permute-start.2) | collective-permute-done | bytes 224 | tf_op jit(solution)/shard_map/ppermute | solution.py:17
  39.6 10.8 %gather_fusion.3 = f32[4096,3]{1,0:T(8,128)S(1)} fusion(f32[3,288]{0,1:T(8,128)S(1)} %pad_maximum_fusion, s32[4096]{0:T(1024)S(1)} %broadcast_clamp_fusion.1), kind=kCustom, calls=%fused_computation.7 | custom fusion | bytes 114688 | tf_op jit(solution)/shard_map/jvp(jit(_take))/gather | solution.py:46
  59.8 10.8 %gather_fusion.6 = f32[4096,128]{1,0:T(8,128)S(1)} fusion(f32[288,128]{1,0:T(8,128)S(1)} %pad_maximum_fusion.1, s32[4096]{0:T(1024)S(1)} %broadcast_clamp_fusion.1), kind=kCustom, calls=%fused_computation.10 | custom fusion | bytes 4210688 | tf_op jit(solution)/shard_map/jvp(jit(_take))/gather | solution.py:59
  70.7 5.7 %multiply_convert_fusion = (bf16[32,128,128]{2,1,0:T(8,128)(2,1)S(1)}, f32[32,128,128]{2,1,0:T(8,128)}) fusion(f32[32,128,128]{2,1,0:T(8,128)S(1)} %bitcast.233, pred[32,128]{1,0:T(8,128)(4,1)S(1)} %compare_and_fusion, f32[128,128]{1,0:T(8,128)S(1)} %fusion.47, f32[8,128]{1,0:T(8,128)S(1)} %copy-done.43, f32[32,128]{1,0:T(8,128)S(1)} %get-tuple-element.447, ...), kind=kOutput, calls=%fused_computation.48 | convolution fusion | flops 54624256 | bytes 5333024 | tf_op jit(solution)/shard_map/jvp(nka,nc->kac)/dot_general | solution.py:58
  83.7 107.5 %while.33 = (s32[]{:T(128)}, f32[288,1152]{1,0:T(8,128)S(1)}, f32[4,1024,1,128]{1,3,2,0:T(8,128)}, f32[4,1024,9,1]{1,2,3,0:T(8,128)}, s32[4,1024,1]{1,2,0:T(1,12...) while((s32[]{:T(128)}, f32[288,1152]{1,0:T(8,128)S(1)}, ...), condition=%wide.region_3.4_spmd, body=%wide.region_1.3_spmd.sunk | while | flops 2359298 | bytes 31389316 | solution.py:88
  89.1 6.1 %copy.616 = f32[1024,1152]{1,0:T(8,128)} copy(f32[1024,1152]{0,1:T(8,128)} %bitcast.215) | data formatting | bytes 9437184 | tf_op jit(solution)/shard_map/jvp()/while/body/eval_jaxpr/mul | solution.py:82
  95.3 11.4 %scatter_fusion = f32[288,1152]{1,0:T(8,128)S(1)} fusion(f32[288,1152]{1,0:T(8,128)S(1)} %get-tuple-element.575, s32[1024]{0:T(1024)S(1)} %bitcast.241, f32[1024,1152]{1,0:T(8,128)} %copy.616), kind=kCustom, calls=%fused_computation.11.clone.1 | custom fusion | flops 1179648 | bytes 14159872 | tf_op jit(solution)/shard_map/jvp()/while/body/eval_jaxpr/scatter-add | solution.py:85
  116.0 6.1 %copy.616 = f32[1024,1152]{1,0:T(8,128)} copy(f32[1024,1152]{0,1:T(8,128)} %bitcast.215) | data formatting | bytes 9437184 | tf_op jit(solution)/shard_map/jvp()/while/body/eval_jaxpr/mul | solution.py:82
  122.1 11.4 %scatter_fusion = f32[288,1152]{1,0:T(8,128)S(1)} fusion(f32[288,1152]{1,0:T(8,128)S(1)} %get-tuple-element.575, s32[1024]{0:T(1024)S(1)} %bitcast.241, f32[1024,1152]{1,0:T(8,128)} %copy.616), kind=kCustom, calls=%fused_computation.11.clone.1 | custom fusion | flops 1179648 | bytes 14159872 | tf_op jit(solution)/shard_map/jvp()/while/body/eval_jaxpr/scatter-add | solution.py:85
  142.8 6.1 %copy.616 = f32[1024,1152]{1,0:T(8,128)} copy(f32[1024,1152]{0,1:T(8,128)} %bitcast.215) | data formatting | bytes 9437184 | tf_op jit(solution)/shard_map/jvp()/while/body/eval_jaxpr/mul | solution.py:82
  149.0 11.4 %scatter_fusion = f32[288,1152]{1,0:T(8,128)S(1)} fusion(f32[288,1152]{1,0:T(8,128)S(1)} %get-tuple-element.575, s32[1024]{0:T(1024)S(1)} %bitcast.241, f32[1024,1152]{1,0:T(8,128)} %copy.616), kind=kCustom, calls=%fused_computation.11.clone.1 | custom fusion | flops 1179648 | bytes 14159872 | tf_op jit(solution)/shard_map/jvp()/while/body/eval_jaxpr/scatter-add | solution.py:85
  169.7 6.1 %copy.616 = f32[1024,1152]{1,0:T(8,128)} copy(f32[1024,1152]{0,1:T(8,128)} %bitcast.215) | data formatting | bytes 9437184 | tf_op jit(solution)/shard_map/jvp()/while/body/eval_jaxpr/mul | solution.py:82
  175.9 11.4 %scatter_fusion = f32[288,1152]{1,0:T(8,128)S(1)} fusion(f32[288,1152]{1,0:T(8,128)S(1)} %get-tuple-element.575, s32[1024]{0:T(1024)S(1)} %bitcast.241, f32[1024,1152]{1,0:T(8,128)} %copy.616), kind=kCustom, calls=%fused_computation.11.clone.1 | custom fusion | flops 1179648 | bytes 14159872 | tf_op jit(solution)/shard_map/jvp()/while/body/eval_jaxpr/scatter-add | solution.py:85
  198.0 4.9 fusion.10
  237.0 5.8 %collective-permute-start.12 = (f32[64,1152]{1,0:T(8,128)}, f32[64,1152]{1,0:T(8,128)}, u32[]{:S(2)}, u32[]{:S(2)}) collective-permute-start(f32[64,1152]{1,0:T(8,128)} %broadcast_select_fusion.1), channel_id=1, source_target_pairs={{8,0},{16,8},{24,16},{32,24},{40,32},{48,40},{56,48},{64,56},{72,6... | collective-permute-start | bytes 884744 | tf_op jit(solution)/shard_map/ppermute | solution.py:17
  248.1 5.7 %collective-permute-start.13 = (f32[64,1152]{1,0:T(8,128)}, f32[64,1152]{1,0:T(8,128)}, u32[]{:S(2)}, u32[]{:S(2)}) collective-permute-start(f32[64,1152]{1,0:T(8,128)} %broadcast_select_fusion), channel_id=1, source_target_pairs={{1,0},{2,1},{3,2},{4,3},{5,4},{6,5},{7,6},{0,7},{9,8},{10,9},{11,1... | collective-permute-start | bytes 884744 | tf_op jit(solution)/shard_map/ppermute | solution.py:17
  256.7 6.6 %fusion.9 = f32[128,9,32]{2,1,0:T(8,128)} fusion(f32[128,9,128]{2,1,0:T(8,128)} %copy.549, f32[32,128,128]{2,1,0:T(8,128)S(1)} %bitcast.219, f32[32,128]{0,1:T(8,128)S(1)} %copy-done.13), kind=kOutput, calls=%fused_computation.52 | convolution fusion | flops 57147392 | bytes 2850816 | tf_op jit(solution)/shard_map/transpose(jvp(mka,kac->amc))/dot_general | solution.py:68
  276.4 77.4 %while.34 = (s32[]{:T(128)}, f32[4,9,1024]{2,1,0:T(8,128)}, f32[4,1024,128]{2,1,0:T(8,128)}, s32[4,1024,1]{1,2,0:T(1,128)}, f32[288,1152]{1,0:T(8,128)S(1)}, /*i...) while((s32[]{:T(128)}, f32[4,9,1024]{2,1,0:T(8,128)}, ...), condition=%wide.region_13.16_spmd, body=%wide.region_10.15_spmd.sunk | while | flops 5762051 | bytes 28059772 | solution.py:88
  277.2 5.7 %gather_fusion = f32[1024,1152]{1,0:T(8,128)} fusion(f32[288,1152]{1,0:T(8,128)S(1)} %get-tuple-element.614, s32[1024]{0:T(1024)S(1)} %broadcast_clamp_fusion.3), kind=kCustom, calls=%fused_computation.2.clone.1 | custom fusion | bytes 9441280 | tf_op jit(solution)/shard_map/transpose(jvp())/while/body/eval_jaxpr/gather | solution.py:85
  282.9 6.1 %copy.617 = f32[1024,1152]{0,1:T(8,128)} copy(f32[1024,1152]{1,0:T(8,128)} %gather_fusion) | data formatting | bytes 9437184 | tf_op jit(solution)/shard_map/transpose(jvp())/while/body/eval_jaxpr/gather | solution.py:85
  296.6 5.7 %gather_fusion = f32[1024,1152]{1,0:T(8,128)} fusion(f32[288,1152]{1,0:T(8,128)S(1)} %get-tuple-element.614, s32[1024]{0:T(1024)S(1)} %broadcast_clamp_fusion.3), kind=kCustom, calls=%fused_computation.2.clone.1 | custom fusion | bytes 9441280 | tf_op jit(solution)/shard_map/transpose(jvp())/while/body/eval_jaxpr/gather | solution.py:85
  302.2 6.1 %copy.617 = f32[1024,1152]{0,1:T(8,128)} copy(f32[1024,1152]{1,0:T(8,128)} %gather_fusion) | data formatting | bytes 9437184 | tf_op jit(solution)/shard_map/transpose(jvp())/while/body/eval_jaxpr/gather | solution.py:85
  315.9 5.7 %gather_fusion = f32[1024,1152]{1,0:T(8,128)} fusion(f32[288,1152]{1,0:T(8,128)S(1)} %get-tuple-element.614, s32[1024]{0:T(1024)S(1)} %broadcast_clamp_fusion.3), kind=kCustom, calls=%fused_computation.2.clone.1 | custom fusion | bytes 9441280 | tf_op jit(solution)/shard_map/transpose(jvp())/while/body/eval_jaxpr/gather | solution.py:85
  321.5 6.1 %copy.617 = f32[1024,1152]{0,1:T(8,128)} copy(f32[1024,1152]{1,0:T(8,128)} %gather_fusion) | data formatting | bytes 9437184 | tf_op jit(solution)/shard_map/transpose(jvp())/while/body/eval_jaxpr/gather | solution.py:85
  335.2 5.7 %gather_fusion = f32[1024,1152]{1,0:T(8,128)} fusion(f32[288,1152]{1,0:T(8,128)S(1)} %get-tuple-element.614, s32[1024]{0:T(1024)S(1)} %broadcast_clamp_fusion.3), kind=kCustom, calls=%fused_computation.2.clone.1 | custom fusion | bytes 9441280 | tf_op jit(solution)/shard_map/transpose(jvp())/while/body/eval_jaxpr/gather | solution.py:85
  340.9 6.1 %copy.617 = f32[1024,1152]{0,1:T(8,128)} copy(f32[1024,1152]{1,0:T(8,128)} %gather_fusion) | data formatting | bytes 9437184 | tf_op jit(solution)/shard_map/transpose(jvp())/while/body/eval_jaxpr/gather | solution.py:85
  357.6 8.8 %broadcast_multiply_fusion.1 = (f32[32,128,128]{2,0,1:T(8,128)S(1)}, f32[32,128]{0,1:T(8,128)S(1)}) fusion(f32[32,128]{0,1:T(8,128)} %copy.525, f32[32,128,128]{2,1,0:T(8,128)} %bitcast.220, f32[128,9,128]{2,1,0:T(8,128)S(1)} %copy-done.5, f32[9,32,128]{1,0,2:T(8,128)S(1)} %copy-done.4, f32[32,128,128]{2,1,0:T(8,128)} %bitcast.223), kind=kOutput, calls=%fused_computation.59 | convolution fusion | flops 58716160 | bytes 7061504 | tf_op jit(solution)/shard_map/transpose(jvp(mka,kac->amc))/dot_general | solution.py:68
  377.0 22.8 %scatter_fusion.1 = f32[3,288]{0,1:T(8,128)S(1)} fusion(f32[3,288]{0,1:T(8,128)S(1)} %pad.29, s32[4096]{0:T(1024)S(1)} %copy-done.26, f32[4096,3]{1,0:T(8,128)S(1)} %bitcast.231), kind=kCustom, calls=%fused_computation.13 | custom fusion | flops 12288 | bytes 163840 | tf_op jit(solution)/shard_map/transpose(jvp(jit(_take)))/scatter-add | solution.py:46
  399.9 5.1 %collective-permute-start.19 = (f32[3,16]{0,1:T(8,128)S(1)}, f32[3,16]{0,1:T(8,128)S(1)}, u32[]{:S(2)}, u32[]{:S(2)}) collective-permute-start(f32[3,16]{0,1:T(8,128)S(1)} %slice.193), channel_id=1, source_target_pairs={{1,0},{2,1},{3,2},{4,3},{5,4},{6,5},{7,6},{0,7},{9,8},{10,9},{11,1... | collective-permute-start | bytes 584 | tf_op jit(solution)/shard_map/ppermute | solution.py:17
  410.0 77.2 %all-reduce.7 = (f32[]{:T(128)}, f32[]{:T(128)}) all-reduce(f32[]{:T(128)} %fusion.25, f32[]{:T(128)S(6)} %convert_element_type.37), channel_id=1, replica_groups=mesh['gx'=32,'gy'=8] {'gx','gy'}, use_global_device_ids=true, to_apply=%region_8.9 | all-reduce | flops 2 | bytes 16 | tf_op jit(solution)/shard_map/psum | solution.py:235
  (381 shorter events, 190.3 us)
Async XLA Ops:
  0.6 223.0 %copy-start = (bf16[384,128]{1,0:T(8,128)(2,1)S(1)}, bf16[384,128]{1,0:T(8,128)(2,1)}, u32[]{:S(2)}) copy-start(bf16[384,128]{1,0:T(8,128)(2,1)} %param.35) | copy-start | bytes 294916
  4.5 21.0 %collective-permute-start = (f32[3,96]{0,1:T(8,128)S(1)}, f32[3,96]{0,1:T(8,128)S(1)}, u32[]{:S(2)}, u32[]{:S(2)}) collective-permute-start(f32[3,96]{0,1:T(8,128)S(1)} %select_bitcast_fusion), channel_id=1, source_target_pairs={{8,0},{16,8},{24,16},{32,24},{40,32},{48,40},{56,48},{64,56},{72,6... | collective-permute-start | bytes 3464 | tf_op jit(solution)/shard_map/ppermute | solution.py:17
  9.4 43.4 %collective-permute-start.3 = (f32[96,128]{1,0:T(8,128)S(1)}, f32[96,128]{1,0:T(8,128)S(1)}, u32[]{:S(2)}, u32[]{:S(2)}) collective-permute-start(f32[96,128]{1,0:T(8,128)S(1)} %broadcast_select_fusion.4), channel_id=1, source_target_pairs={{8,0},{16,8},{24,16},{32,24},{40,32},{48,40},{56,48},{64,56},{72,6... | collective-permute-start | bytes 147464 | tf_op jit(solution)/shard_map/ppermute | solution.py:17
  16.8 53.8 %copy-start.18 = (pred[32,128]{1,0:T(8,128)(4,1)}, pred[32,128]{1,0:T(8,128)(4,1)S(1)}, u32[]{:S(2)}) copy-start(pred[32,128]{1,0:T(8,128)(4,1)S(1)} %compare_and_fusion) | copy-start | bytes 12292
  17.4 33.6 %copy-start.31 = (s32[1,1,128]{2,1,0:T(1,128)S(1)}, s32[1,1,128]{2,1,0:T(1,128)}, u32[]{:S(2)}) copy-start(s32[1,1,128]{2,1,0:T(1,128)} %param.27) | copy-start | bytes 1540
  18.1 52.6 %copy-start.48 = (f32[8]{0:T(128)}, f32[8]{0:T(128)S(1)}, u32[]{:S(2)}) copy-start(f32[8]{0:T(128)S(1)} %convert_multiply_fusion.2) | copy-start | bytes 100
  22.4 48.2 %copy-start.21 = (f32[128,128]{1,0:T(8,128)}, f32[128,128]{1,0:T(8,128)S(1)}, u32[]{:S(2)}) copy-start(f32[128,128]{1,0:T(8,128)S(1)} %fusion.47) | copy-start | bytes 196612
  25.6 13.1 %collective-permute-start.1 = (f32[3,80]{0,1:T(8,128)S(1)}, f32[3,80]{0,1:T(8,128)S(1)}, u32[]{:S(2)}, u32[]{:S(2)}) collective-permute-start(f32[3,80]{0,1:T(8,128)S(1)} %pad_maximum_fusion.3), channel_id=1, source_target_pairs={{1,0},{2,1},{3,2},{4,3},{5,4},{6,5},{7,6},{0,7},{9,8},{10,9},{11,1... | collective-permute-start | bytes 2888 | tf_op jit(solution)/shard_map/ppermute | solution.py:17
  32.4 6.2 %collective-permute-start.2 = (f32[3,16]{0,1:T(8,128)S(1)}, f32[3,16]{0,1:T(8,128)S(1)}, u32[]{:S(2)}, u32[]{:S(2)}) collective-permute-start(f32[3,16]{0,1:T(8,128)S(1)} %get-tuple-element.443), channel_id=1, source_target_pairs={{7,0},{0,1},{1,2},{2,3},{3,4},{4,5},{5,6},{6,7},{15,8},{8,9},{9,10... | collective-permute-start | bytes 584 | tf_op jit(solution)/shard_map/ppermute | solution.py:17
  52.9 6.9 %collective-permute-start.4 = (f32[80,128]{1,0:T(8,128)S(1)}, f32[80,128]{1,0:T(8,128)S(1)}, u32[]{:S(2)}, u32[]{:S(2)}) collective-permute-start(f32[80,128]{1,0:T(8,128)S(1)} %pad_maximum_fusion.4), channel_id=1, source_target_pairs={{1,0},{2,1},{3,2},{4,3},{5,4},{6,5},{7,6},{0,7},{9,8},{10,9},{11,1... | collective-permute-start | bytes 122888 | tf_op jit(solution)/shard_map/ppermute | solution.py:17
  52.9 6.8 %collective-permute-start.5 = (f32[16,128]{1,0:T(8,128)S(1)}, f32[16,128]{1,0:T(8,128)S(1)}, u32[]{:S(2)}, u32[]{:S(2)}) collective-permute-start(f32[16,128]{1,0:T(8,128)S(1)} %get-tuple-element.441), channel_id=1, source_target_pairs={{7,0},{0,1},{1,2},{2,3},{3,4},{4,5},{5,6},{6,7},{15,8},{8,9},{9,10... | collective-permute-start | bytes 24584 | tf_op jit(solution)/shard_map/ppermute | solution.py:17
  78.3 178.4 %copy-start.2 = (f32[4096,128]{1,0:T(8,128)}, f32[4096,128]{1,0:T(8,128)S(1)}, u32[]{:S(2)}) copy-start(f32[4096,128]{1,0:T(8,128)S(1)} %get-tuple-element.461) | copy-start | bytes 6291460
  192.7 20.1 %collective-permute-start.6 = (f32[64,1152]{1,0:T(8,128)}, f32[64,1152]{1,0:T(8,128)}, u32[]{:S(2)}, u32[]{:S(2)}) collective-permute-start(f32[64,1152]{1,0:T(8,128)} %get-tuple-element.424), channel_id=1, source_target_pairs={{248,0},{0,8},{8,16},{16,24},{24,32},{32,40},{40,48},{48,56},{56,6... | collective-permute-start | bytes 884744 | tf_op jit(solution)/shard_map/ppermute | solution.py:17
  192.7 20.1 %collective-permute-start.7 = (f32[64,1152]{1,0:T(8,128)}, f32[64,1152]{1,0:T(8,128)}, u32[]{:S(2)}, u32[]{:S(2)}) collective-permute-start(f32[64,1152]{1,0:T(8,128)} %get-tuple-element.425), channel_id=1, source_target_pairs={{7,0},{0,1},{1,2},{2,3},{3,4},{4,5},{5,6},{6,7},{15,8},{8,9},{9,10... | collective-permute-start | bytes 884744 | tf_op jit(solution)/shard_map/ppermute | solution.py:17
  193.4 13.9 %collective-permute-start.10 = (f32[16,1152]{1,0:T(8,128)}, f32[16,1152]{1,0:T(8,128)}, u32[]{:S(2)}, u32[]{:S(2)}) collective-permute-start(f32[16,1152]{1,0:T(8,128)} %get-tuple-element.427), channel_id=1, source_target_pairs={{1,0},{2,1},{3,2},{4,3},{5,4},{6,5},{7,6},{0,7},{9,8},{10,9},{11,1... | collective-permute-start | bytes 221192 | tf_op jit(solution)/shard_map/ppermute | solution.py:17
  197.8 10.7 %collective-permute-start.8 = (f32[16,1152]{1,0:T(8,128)}, f32[16,1152]{1,0:T(8,128)}, u32[]{:S(2)}, u32[]{:S(2)}) collective-permute-start(f32[16,1152]{1,0:T(8,128)} %get-tuple-element.426), channel_id=1, source_target_pairs={{7,0},{0,1},{1,2},{2,3},{3,4},{4,5},{5,6},{6,7},{15,8},{8,9},{9,10... | collective-permute-start | bytes 221192 | tf_op jit(solution)/shard_map/ppermute | solution.py:17
  207.3 5.4 %collective-permute-start.11 = (f32[16,1152]{1,0:T(8,128)}, f32[16,1152]{1,0:T(8,128)}, u32[]{:S(2)}, u32[]{:S(2)}) collective-permute-start(f32[16,1152]{1,0:T(8,128)} %collective-permute-done.10), channel_id=1, source_target_pairs={{248,0},{0,8},{8,16},{16,24},{24,32},{32,40},{40,48},{48,56},{56,6... | collective-permute-start | bytes 221192 | tf_op jit(solution)/shard_map/ppermute | solution.py:17
  208.5 4.4 collective-permute-start.9
  237.0 29.7 %collective-permute-start.12 = (f32[64,1152]{1,0:T(8,128)}, f32[64,1152]{1,0:T(8,128)}, u32[]{:S(2)}, u32[]{:S(2)}) collective-permute-start(f32[64,1152]{1,0:T(8,128)} %broadcast_select_fusion.1), channel_id=1, source_target_pairs={{8,0},{16,8},{24,16},{32,24},{40,32},{48,40},{56,48},{64,56},{72,6... | collective-permute-start | bytes 884744 | tf_op jit(solution)/shard_map/ppermute | solution.py:17
  245.1 8.6 %collective-permute-start.14 = (f32[16,1152]{1,0:T(8,128)S(1)}, f32[16,1152]{1,0:T(8,128)}, u32[]{:S(2)}, u32[]{:S(2)}) collective-permute-start(f32[16,1152]{1,0:T(8,128)S(1)} %broadcast_select_fusion.3), channel_id=1, source_target_pairs={{8,0},{16,8},{24,16},{32,24},{40,32},{48,40},{56,48},{64,56},{72,6... | collective-permute-start | bytes 221192 | tf_op jit(solution)/shard_map/ppermute | solution.py:17
  246.1 7.7 %collective-permute-start.16 = (f32[16,1152]{1,0:T(8,128)S(1)}, f32[16,1152]{1,0:T(8,128)}, u32[]{:S(2)}, u32[]{:S(2)}) collective-permute-start(f32[16,1152]{1,0:T(8,128)S(1)} %broadcast_select_fusion.2), channel_id=1, source_target_pairs={{8,0},{16,8},{24,16},{32,24},{40,32},{48,40},{56,48},{64,56},{72,6... | collective-permute-start | bytes 221192 | tf_op jit(solution)/shard_map/ppermute | solution.py:17
  248.1 20.7 %collective-permute-start.13 = (f32[64,1152]{1,0:T(8,128)}, f32[64,1152]{1,0:T(8,128)}, u32[]{:S(2)}, u32[]{:S(2)}) collective-permute-start(f32[64,1152]{1,0:T(8,128)} %broadcast_select_fusion), channel_id=1, source_target_pairs={{1,0},{2,1},{3,2},{4,3},{5,4},{6,5},{7,6},{0,7},{9,8},{10,9},{11,1... | collective-permute-start | bytes 884744 | tf_op jit(solution)/shard_map/ppermute | solution.py:17
  253.7 11.7 %collective-permute-start.15 = (f32[16,1152]{1,0:T(8,128)}, f32[16,1152]{1,0:T(8,128)S(1)}, u32[]{:S(2)}, u32[]{:S(2)}) collective-permute-start(f32[16,1152]{1,0:T(8,128)} %collective-permute-done.14), channel_id=1, source_target_pairs={{1,0},{2,1},{3,2},{4,3},{5,4},{6,5},{7,6},{0,7},{9,8},{10,9},{11,1... | collective-permute-start | bytes 221192 | tf_op jit(solution)/shard_map/ppermute | solution.py:17
  253.8 11.8 %collective-permute-start.17 = (f32[16,1152]{1,0:T(8,128)}, f32[16,1152]{1,0:T(8,128)S(1)}, u32[]{:S(2)}, u32[]{:S(2)}) collective-permute-start(f32[16,1152]{1,0:T(8,128)} %collective-permute-done.16), channel_id=1, source_target_pairs={{7,0},{0,1},{1,2},{2,3},{3,4},{4,5},{5,6},{6,7},{15,8},{8,9},{9,10... | collective-permute-start | bytes 221192 | tf_op jit(solution)/shard_map/ppermute | solution.py:17
  276.4 78.7 %copy-start.39 = (f32[9]{0:T(128)S(1)}, f32[9]{0:T(128)}, u32[]{:S(2)}) copy-start(f32[9]{0:T(128)} %constant.275.clone) | copy-start | bytes 112
  276.4 81.2 %copy-start.5 = (f32[128,9,128]{2,1,0:T(8,128)S(1)}, f32[128,9,128]{2,1,0:T(8,128)}, u32[]{:S(2)}) copy-start(f32[128,9,128]{2,1,0:T(8,128)} %copy.549) | copy-start | bytes 1769476
  376.0 33.2 %copy-start.25 = (f32[128,128]{1,0:T(8,128)S(1)}, f32[128,128]{1,0:T(8,128)}, u32[]{:S(2)}) copy-start(f32[128,128]{1,0:T(8,128)} %copy-done.24) | copy-start | bytes 196612
  376.1 114.9 %copy-start.1 = (bf16[384,128]{1,0:T(8,128)(2,1)S(1)}, bf16[384,128]{1,0:T(8,128)(2,1)}, u32[]{:S(2)}) copy-start(bf16[384,128]{1,0:T(8,128)(2,1)} %param.35) | copy-start | bytes 294916
  376.1 112.8 %copy-start.35 = (s32[160,1]{0,1:T(1,128)S(1)}, s32[160,1]{0,1:T(1,128)}, u32[]{:S(2)}) copy-start(s32[160,1]{0,1:T(1,128)} %compare_select_fusion.2) | copy-start | bytes 1924
  399.8 6.5 %collective-permute-start.18 = (f32[3,80]{0,1:T(8,128)S(1)}, f32[3,80]{0,1:T(8,128)S(1)}, u32[]{:S(2)}, u32[]{:S(2)}) collective-permute-start(f32[3,80]{0,1:T(8,128)S(1)} %slice.191), channel_id=1, source_target_pairs={{7,0},{0,1},{1,2},{2,3},{3,4},{4,5},{5,6},{6,7},{15,8},{8,9},{9,10... | collective-permute-start | bytes 2888 | tf_op jit(solution)/shard_map/ppermute | solution.py:17
  399.9 5.9 %collective-permute-start.19 = (f32[3,16]{0,1:T(8,128)S(1)}, f32[3,16]{0,1:T(8,128)S(1)}, u32[]{:S(2)}, u32[]{:S(2)}) collective-permute-start(f32[3,16]{0,1:T(8,128)S(1)} %slice.193), channel_id=1, source_target_pairs={{1,0},{2,1},{3,2},{4,3},{5,4},{6,5},{7,6},{0,7},{9,8},{10,9},{11,1... | collective-permute-start | bytes 584 | tf_op jit(solution)/shard_map/ppermute | solution.py:17
  406.5 82.1 %collective-permute-start.20 = (f32[3,96]{1,0:T(4,128)S(1)}, f32[3,96]{1,0:T(4,128)S(1)}, u32[]{:S(2)}, u32[]{:S(2)}) collective-permute-start(f32[3,96]{1,0:T(4,128)S(1)} %pad_maximum_fusion.5), channel_id=1, source_target_pairs={{248,0},{0,8},{8,16},{16,24},{24,32},{32,40},{40,48},{48,56},{56,6... | collective-permute-start | bytes 3464 | tf_op jit(solution)/shard_map/ppermute | solution.py:17
  (43 other events, 286.6 us)
where the time goes:
time: 501 us; the launch traced here: 492 us
  local copies, waits for them, and re-layouts  183 us (37%)
  other arithmetic  135 us (27%)
  blocking collectives  77.2 us (15%)
  starting transfers between devices  44.3 us (9%)
  matrix products  36 us (7%)
  waiting for transfers between devices  11.5 us (2%)
    psum x1, blocking collectives, on_device(): lax.psum((local_total, live_count.astype(jnp.float32)), ('gx', 'gy'))  77.2 us
    gather x8, local copies, waits for them, and re-layouts, add_block(): jax.ops.segment_sum(term, index_block, num_segments=total_rows)  47.1 us
    scatter-add x4, other arithmetic, add_block(): jax.ops.segment_sum(term, index_block, num_segments=total_rows)  45.6 us
    ppermute x21, starting transfers between devices, from_behind(): return lax.ppermute(block, axis, route)  44.3 us
    mul x16, local copies, waits for them, and re-layouts, add_block(): jnp.transpose(harm_block)[:, :, None] * weight_block[:, None, :]  36.6 us
    scatter-add x1, other arithmetic, pair_terms(): other = jnp.take(placed, nbr_index, axis=1)  22.8 us
    dynamic_update_slice x24, local copies, waits for them, and re-layouts, pair_terms(): lax.scan(add_block, start, (signed, weight_blocks, index_blocks))  22.3 us
    dot_general x3, matrix products, pair_terms(): jnp.einsum('mka,kac->amc', harm, weight, precision=lax.Precision.HIGHEST)  20.2 us
  transfers between devices with their start and end apart: 21, of which 7 were waited for; matrix products, arithmetic and copies ran while one was open for 12% of the time, Pallas kernels for 0%

commit v1 on v0

v1 whole, which is shorter than its diff:
```python
import functools
import math

import jax
import jax.numpy as jnp
from jax import lax
from jax.experimental import pallas as pl
from jax.experimental.pallas import tpu as pltpu
from jax.sharding import PartitionSpec as P

cutoff = 6.0
soften = 0.25
box_width = 4.0
f32 = jnp.float32
bf16 = jnp.bfloat16
MESH = pl.DeviceIdType.MESH

A = 128
C = 128
K = 32
GF = 64
GC = 16
NG = 2 * GF + 2 * GC
R = A + NG
NB = 8
PAIRS = K * A
STEP = 4
WIDE = STEP * A
ORDER = (0, 4, 5, 6, 7, 8, 1, 2, 3)
CHUNKS = ((0, 2), (2, 4), (4, 6), (6, 9))
GROUPS = ((0, GF), (GF, GF), (2 * GF, GC), (2 * GF + GC, GC))


def dot(a, b):
    return lax.dot_general(a, b, (((1,), (0,)), ((), ())), preferred_element_type=f32)


def dot_nt(a, b):
    return lax.dot_general(a, b, (((1,), (1,)), ((), ())), preferred_element_type=f32)


def split(x):
    hi = x.astype(bf16)
    lo = (x - hi.astype(f32)).astype(bf16)
    return hi, lo


def silu_parts(x):
    s = 0.5 + 0.5 * jnp.tanh(0.5 * x)
    y = x * s
    return y, s + y * (1.0 - s)


def pick_lanes(table, index):
    return jnp.take_along_axis(table, index, axis=1)


def kernel(
    sizes,
    feat_ref,
    pos_ref,
    nbr_ref,
    cnt_ref,
    dom_ref,
    face_ref,
    corner_ref,
    wc_ref,
    wn_ref,
    wr_ref,
    wl_ref,
    wo_ref,
    we_ref,
    energy_ref,
    force_ref,
    outf,
    outc,
    inf,
    inc,
    proj,
    left,
    cent,
    even,
    odd,
    brow,
    harm,
    geom,
    lat,
    d1s,
    d2s,
    term,
    mom,
    msend,
    mrecv,
    slope_send,
    slope_recv,
    gt,
    dw,
    dys,
    dbs,
    ddr,
    fsend,
    frecv,
    ebuf_a,
    ebuf_b,
    ebuf_c,
    s1,
    r1,
    s2,
    r2,
    s3,
    r3,
    s4,
    r4,
    sa,
    ra,
    sb,
    rb,
    sc,
    rc,
):
    nx, ny = sizes
    gx = lax.axis_index("gx")
    gy = lax.axis_index("gy")
    up_x, down_x = lax.rem(gx + 1, nx), lax.rem(gx + nx - 1, nx)
    up_y, down_y = lax.rem(gy + 1, ny), lax.rem(gy + ny - 1, ny)
    holders = ((down_x, gy), (gx, down_y), (down_x, down_y), (down_x, up_y))
    owners = ((up_x, gy), (gx, up_y), (up_x, up_y), (up_x, down_y))
    inner = min(nx, 8)
    outer = nx // inner
    block, place = gx // inner, lax.rem(gx, inner)

    def group_a(i):
        return (block * inner + i, gy)

    def group_b(i):
        return (i * inner + place, gy)

    def group_c(i):
        return (gx, i)

    stages = (
        (inner, place, group_a, ebuf_a, sa, ra),
        (outer, block, group_b, ebuf_b, sb, rb),
        (ny, gy, group_c, ebuf_c, sc, rc),
    )

    barrier = pltpu.get_barrier_semaphore()
    greeted = list(holders) + list(owners)
    for count, mine, where, unused_buf, unused_s, unused_r in stages:
        for s in range(1, count):
            greeted.append(where(lax.rem(mine + s, count)))
    for target in greeted:
        pl.semaphore_signal(barrier, inc=1, device_id=target, device_id_type=MESH)

    sub = lax.broadcasted_iota(jnp.int32, (A, A), 0)
    lane = lax.broadcasted_iota(jnp.int32, (A, A), 1)
    eye = jnp.where(sub == lane, 1.0, 0.0)
    lists_a = jnp.concatenate([face_ref[0:1, :], face_ref[1:2, :]], axis=1)
    none = jnp.full((1, A - 2 * GC), -1, jnp.int32)
    lists_b = jnp.concatenate([corner_ref[0:1, :], corner_ref[1:2, :], none], axis=1)
    pt_a = jnp.where(sub == lists_a, 1.0, 0.0)
    pt_b = jnp.where(sub == lists_b, 1.0, 0.0)
    pick = jnp.concatenate([pt_a.T, pt_b.T[0 : 2 * GC]], axis=0).astype(bf16)
    spread = jnp.concatenate([pt_a, pt_b], axis=1).astype(bf16)[:, 0:NG]
    feat = feat_ref[...]
    picked = dot(pick, feat)
    small = lax.broadcasted_iota(jnp.int32, (3, A), 0)
    wide = lax.broadcasted_iota(jnp.int32, (3, A), 1)
    pos = pos_ref[...]
    zero = jnp.zeros((3, A), f32)
    at_a = pick_lanes(pos, jnp.broadcast_to(lists_a, (3, A)))
    at_b = pick_lanes(pos, jnp.broadcast_to(jnp.maximum(lists_b, 0), (3, A)))
    at_a = at_a + jnp.where(small == jnp.where(wide < GF, 0, 1), box_width, zero)
    tilt = jnp.where(wide < GC, box_width, -box_width)
    at_b = at_b + jnp.where(small == 0, box_width, jnp.where(small == 1, tilt, zero))
    for g, (base, rows) in enumerate(GROUPS):
        buf, slot, at = (outf, g, at_a) if g < 2 else (outc, g - 2, at_b)
        buf[slot, 0:rows, :] = picked[base : base + rows]
        buf[slot, rows : rows + 8, :] = jnp.zeros((8, A), f32)
        buf[slot, rows : rows + 3, :] = at

    pl.semaphore_wait(barrier, len(greeted))

    def first_copy(g):
        src, dst, slot = (outf, inf, g) if g < 2 else (outc, inc, g - 2)
        return pltpu.make_async_remote_copy(
            src_ref=src.at[slot],
            dst_ref=dst.at[slot],
            send_sem=s1.at[g],
            recv_sem=r1.at[g],
            device_id=holders[g],
            device_id_type=MESH,
        )

    for g in (1, 3, 2, 0):
        first_copy(g).start()

    proj[0:A, :] = dot(feat, wn_ref[...])
    center = dot(feat, wc_ref[...])
    wr = wr_ref[...]
    wr_hi = wr.astype(bf16).astype(f32)
    proj[R : R + NB, :] = wr_hi
    proj[R + NB : R + 2 * NB, :] = wr_hi
    proj[R + 2 * NB : R + 3 * NB, :] = wr - wr_hi
    proj[R + 3 * NB :, :] = jnp.zeros((384 - R - 3 * NB, C), f32)
    own_t = proj[0:A, :].T.astype(bf16)
    left[:, 0:A] = own_t
    cent[...] = center.T - own_t.astype(f32)

    sub_g = lax.broadcasted_iota(jnp.int32, (NG, A), 0) + A

    def build(k, carry):
        lanes = pl.ds(pl.multiple_of(k * A, A), A)
        index = nbr_ref[pl.ds(k, 1), :]
        own = jnp.where(sub == index, 1.0, 0.0)
        even[0:A, lanes] = (eye + own).astype(bf16)
        odd[0:A, lanes] = (eye - own).astype(bf16)
        ghost = jnp.where(sub_g == index, 1.0, 0.0)
        even[A:R, lanes] = ghost.astype(bf16)
        odd[A:R, lanes] = (-ghost).astype(bf16)
        return carry

    lax.fori_loop(0, K, build, 0)

    for g in range(4):
        first_copy(g).wait_recv()
    for g, (base, rows) in enumerate(GROUPS):
        buf, slot = (inf, g) if g < 2 else (inc, g - 2)
        proj[A + base : A + base + rows, :] = dot(
            buf[slot, 0:rows, :].astype(bf16), wn_ref[...]
        )
    left[:, A : 2 * A] = proj[A : 2 * A, :].T.astype(bf16)
    left[:, 2 * A : 3 * A] = proj[2 * A : 3 * A, :].T.astype(bf16)
    ghost_a = jnp.where(wide < GF, inf[0, GF : GF + 3, :], inf[1, GF : GF + 3, :])
    ghost_b = jnp.where(wide < GC, inc[0, GC : GC + 3, :], inc[1, GC : GC + 3, :])

    nbr = nbr_ref[...]
    in_own = nbr < A
    in_face = nbr < 2 * A
    local = jnp.bitwise_and(nbr, A - 1)
    delta = []
    for c in range(3):
        tables = [
            jnp.broadcast_to(t[c : c + 1, :], (K, A)) for t in (pos, ghost_a, ghost_b)
        ]
        found = [pick_lanes(t, local) for t in tables]
        other = jnp.where(in_own, found[0], jnp.where(in_face, found[1], found[2]))
        delta.append(other - tables[0])
    dx, dy, dz = delta
    radius = jnp.sqrt(dx * dx + dy * dy + dz * dz + soften)
    inv = 1.0 / radius
    ux, uy, uz = dx * inv, dy * inv, dz * inv
    t = jnp.minimum(radius / cutoff, 1.0)
    t2 = t * t
    t5 = t2 * t2 * t
    t6 = t5 * t
    envelope = 1.0 + t6 * (-28.0 + t * (48.0 - 21.0 * t))
    slot_no = lax.broadcasted_iota(jnp.int32, (K, A), 0)
    atom_no = lax.broadcasted_iota(jnp.int32, (K, A), 1)
    alive = jnp.logical_and(slot_no < cnt_ref[...], atom_no < dom_ref[...])
    live = jnp.where(alive, 1.0, 0.0)
    root3, root5, root15 = math.sqrt(3.0), math.sqrt(5.0), math.sqrt(15.0)
    y_all = (
        None,
        root3 * ux,
        root3 * uy,
        root3 * uz,
        root15 * ux * uy,
        root15 * uy * uz,
        0.5 * root5 * (3.0 * uz * uz - 1.0),
        root15 * ux * uz,
        0.5 * root15 * (ux * ux - uy * uy),
    )
    for q, m in enumerate(ORDER):
        if m:
            harm[q] = y_all[m]
    geom[0] = envelope * live
    geom[1] = live * (t5 * (-168.0 + t * (336.0 - 168.0 * t)) * jnp.where(radius < cutoff, 1.0 / cutoff, 0.0))
    geom[2], geom[3], geom[4], geom[5] = inv, ux, uy, uz
    theta = radius * (math.pi / cutoff)
    sin1, cos1 = jnp.sin(theta), jnp.cos(theta)
    norm = math.sqrt(2.0 / cutoff)
    s_old, s_now = jnp.zeros_like(theta), sin1
    c_old, c_now = jnp.ones_like(theta), cos1
    for n in range(1, NB + 1):
        value = norm * s_now * inv
        brow[pl.ds(n - 1, K, stride=NB), :] = value
        geom[5 + n] = norm * (n * math.pi / cutoff) * c_now * inv - value * inv
        s_old, s_now = s_now, 2.0 * cos1 * s_now - s_old
        c_old, c_now = c_now, 2.0 * cos1 * c_now - c_old

    def put_basis(k, carry):
        lanes = pl.ds(pl.multiple_of(k * A, A), A)
        tile = brow[pl.ds(pl.multiple_of(k * NB, NB), NB), :]
        hi = tile.astype(bf16).astype(f32)
        rows = jnp.concatenate([hi, tile - hi, hi, jnp.zeros_like(hi)], axis=0)
        even[R : R + 4 * NB, lanes] = rows.astype(bf16)
        return carry

    lax.fori_loop(0, K, put_basis, 0)

    wl_t = wl_ref[...].astype(f32).T.astype(bf16)
    cent_wide = jnp.concatenate([cent[...]] * STEP, axis=1)

    def forward(q, carry):
        lanes = pl.ds(pl.multiple_of(q * WIDE, WIDE), WIDE)
        pre = dot(left[:, 0 : R + 4 * NB], even[:, lanes]) + cent_wide
        hidden, d1 = silu_parts(pre)
        d1s[:, lanes] = d1
        latent, d2 = silu_parts(dot(wl_t, hidden.astype(bf16)))
        lat[:, lanes] = latent
        d2s[:, lanes] = d2
        for s in range(STEP):
            k = q * STEP + s
            cols = pl.ds(pl.multiple_of(k * A, A), A)
            w = latent[:, s * A : (s + 1) * A] * geom[0, pl.ds(k, 1), :]
            for at, m in enumerate(ORDER):
                value = w * harm[at, pl.ds(k, 1), :] if m else w
                term[at * C : (at + 1) * C, cols] = value.astype(bf16)
        return carry

    lax.fori_loop(0, K // STEP, forward, 0)

    def group_copy(src, dst, send, recv, g, part, targets):
        base, rows = GROUPS[g]
        first, last = CHUNKS[part]
        view = (pl.ds(base, rows), pl.ds(first * C, (last - first) * C))
        sem = part * 4 + g
        return pltpu.make_async_remote_copy(
            src_ref=src.at[view],
            dst_ref=dst.at[view],
            send_sem=send.at[sem],
            recv_sem=recv.at[sem],
            device_id=targets[g],
            device_id_type=MESH,
        )

    def moment_copy(g, part):
        return group_copy(msend, mrecv, s2, r2, g, part, owners)

    def slope_copy(g, part):
        return group_copy(slope_send, slope_recv, s3, r3, g, part, holders)

    for part, (first, last) in enumerate(CHUNKS):
        cols = slice(first * C, last * C)
        side = even if first < 6 else odd
        found = dot_nt(side[0:R, :], term[cols, :])
        mom[:, cols] = found[0:A]
        msend[:, cols] = found[A:R]
        for g in (1, 3, 2, 0):
            moment_copy(g, part).start()

    spread2 = jnp.concatenate([spread, spread], axis=1)
    for part, (first, last) in enumerate(CHUNKS):
        cols = slice(first * C, last * C)
        for g in range(4):
            moment_copy(g, part).wait_recv()
        hi, lo = split(mrecv[:, cols])
        mom[:, cols] = mom[:, cols] + dot(spread2, jnp.concatenate([hi, lo], axis=0))

    levels = ((0, 1), (6, 9), (1, 6))
    sums = []
    for first, last in levels:
        total = None
        for at in range(first, last):
            value = mom[:, at * C : (at + 1) * C]
            total = value * value if total is None else total + value * value
        sums.append(total)
    packed = jnp.concatenate([jnp.log1p(x) for x in sums], axis=1).astype(bf16)
    inner_act = dot(packed, wo_ref[...])
    act, d_act = silu_parts(inner_act)
    row_live = jnp.where(sub < dom_ref[...], 1.0, 0.0)
    weighted = row_live * we_ref[...]
    own_energy = jnp.sum(jnp.sum(act * weighted, axis=0, keepdims=True), axis=1, keepdims=True)
    d_inv = dot_nt((d_act * weighted).astype(bf16), wo_ref[...]).astype(bf16).astype(f32)
    pick2 = jnp.concatenate([pick, pick], axis=1)
    scale = [2.0 * d_inv[:, i * C : (i + 1) * C] / (1.0 + sums[i]) for i in range(3)]
    which = (0, 2, 2, 2, 2, 2, 1, 1, 1)
    for part, (first, last) in enumerate(CHUNKS):
        for at in range(first, last):
            cols = slice(at * C, (at + 1) * C)
            value = mom[:, cols] * scale[which[at]]
            hi, lo = split(value)
            slope_send[:, cols] = dot(pick2, jnp.concatenate([hi, lo], axis=0))
            gt[cols, 0:A] = value.T.astype(bf16)
        for g in (1, 3, 2, 0):
            slope_copy(g, part).start()

    def stage_copy(stage, peer, slot):
        count, mine, where, buf, send, recv = stages[stage]
        return pltpu.make_async_remote_copy(
            src_ref=buf.at[mine],
            dst_ref=buf.at[slot],
            send_sem=send.at[peer],
            recv_sem=recv.at[slot],
            device_id=where(peer),
            device_id_type=MESH,
        )

    def stage_start(stage, value):
        count, mine, where, buf, send, recv = stages[stage]
        buf[mine] = value
        for s in range(1, count):
            stage_copy(stage, lax.rem(mine + s, count), mine).start()

    def stage_end(stage):
        count, mine, where, buf, send, recv = stages[stage]
        for s in range(1, count):
            peer = lax.rem(mine + s, count)
            stage_copy(stage, peer, peer).wait_recv()
        total = buf[0]
        for i in range(1, count):
            total = total + buf[i]
        return total

    half = lax.broadcasted_iota(jnp.int32, (8, C), 0)
    pair = jnp.where(half == 0, own_energy, dom_ref[...].astype(f32))
    stage_start(0, pair)

    def pull(q, lo_row, hi_row):
        lanes = pl.ds(pl.multiple_of(q * WIDE, WIDE), WIDE)
        at_even = dot(gt[0 : 6 * C, lo_row:hi_row], even[lo_row:hi_row, lanes])
        at_odd = dot(gt[6 * C : 9 * C, lo_row:hi_row], odd[lo_row:hi_row, lanes])
        outs = []
        for s in range(STEP):
            k = q * STEP + s
            cols = pl.ds(pl.multiple_of(k * A, A), A)
            w = lat[:, cols] * geom[0, pl.ds(k, 1), :]
            total = None
            rows = []
            for at, m in enumerate(ORDER):
                part = at_even if at < 6 else at_odd
                base = (at if at < 6 else at - 6) * C
                h = part[base : base + C, s * A : (s + 1) * A]
                if m:
                    rows.append(jnp.sum(h * w, axis=0, keepdims=True))
                    total = total + h * harm[at, pl.ds(k, 1), :]
                else:
                    total = h
            outs.append((total, rows))
        return outs

    def pull_own(q, carry):
        for s, (total, rows) in enumerate(pull(q, 0, A)):
            k = q * STEP + s
            dw[:, pl.ds(pl.multiple_of(k * A, A), A)] = total
            for at, row in enumerate(rows):
                dys[pl.ds(k * 16 + at, 1), :] = row
        return carry

    lax.fori_loop(0, K // STEP, pull_own, 0)
    stage_start(1, stage_end(0))

    for part, (first, last) in enumerate(CHUNKS):
        for g in range(4):
            slope_copy(g, part).wait_recv()
        for at in range(first, last):
            cols = slice(at * C, (at + 1) * C)
            gt[cols, A : 2 * A] = slope_recv[0:A, cols].T.astype(bf16)
            gt[cols, 2 * A : R] = slope_recv[A:NG, cols].T.astype(bf16)

    wl = wl_ref[...]
    wr2 = jnp.concatenate([wr_hi, wr - wr_hi], axis=0).astype(bf16)

    def pull_ghost(q, carry):
        for s, (total, rows) in enumerate(pull(q, A, R)):
            k = q * STEP + s
            cols = pl.ds(pl.multiple_of(k * A, A), A)
            d_w = dw[:, cols] + total
            for at, row in enumerate(rows):
                spot = pl.ds(k * 16 + at, 1)
                dys[spot, :] = dys[spot, :] + row
            dys[pl.ds(k * 16 + 8, 1), :] = jnp.sum(d_w * lat[:, cols], axis=0, keepdims=True)
            d_pre2 = d_w * geom[0, pl.ds(k, 1), :] * d2s[:, cols]
            d_hidden = dot(wl, d_pre2.astype(bf16)).astype(bf16).astype(f32)
            hi, lo = split(d_hidden * d1s[:, cols])
            two = dot(wr2, hi)
            d_basis = two[0:NB] + two[NB : 2 * NB] + dot(wr2[0:NB], lo)
            dbs[pl.ds(pl.multiple_of(k * NB, NB), NB), :] = d_basis
        return carry

    lax.fori_loop(0, K // STEP, pull_ghost, 0)
    stage_start(2, stage_end(1))

    g_of = {m: dys[pl.ds(at - 1, K, stride=16), :] for at, m in enumerate(ORDER) if m}
    d_radius = dys[pl.ds(8, K, stride=16), :] * geom[1]
    for n in range(1, NB + 1):
        d_radius = d_radius + dbs[pl.ds(n - 1, K, stride=NB), :] * geom[5 + n]
    inv, ux, uy, uz = geom[2], geom[3], geom[4], geom[5]
    dux = root3 * g_of[1] + root15 * (uy * g_of[4] + uz * g_of[7] + ux * g_of[8])
    duy = root3 * g_of[2] + root15 * (ux * g_of[4] + uz * g_of[5] - uy * g_of[8])
    duz = root3 * g_of[3] + root15 * (uy * g_of[5] + ux * g_of[7]) + 3.0 * root5 * uz * g_of[6]
    along = d_radius - (dux * ux + duy * uy + duz * uz) * inv
    for c, (du, u) in enumerate(((dux, ux), (duy, uy), (duz, uz))):
        value = du * inv + u * along
        hi = value.astype(bf16).astype(f32)
        brow[pl.ds(c, K, stride=NB), :] = hi
        brow[pl.ds(c + 3, K, stride=NB), :] = value - hi
    brow[pl.ds(6, K, stride=NB), :] = jnp.zeros((K, A), f32)
    brow[pl.ds(7, K, stride=NB), :] = jnp.zeros((K, A), f32)
    for k in range(K):
        ddr[:, k * A : (k + 1) * A] = brow[k * NB : (k + 1) * NB, :].astype(bf16)
    found = dot_nt(odd[0:R, :], ddr[...])
    wide_found = jnp.concatenate([found, jnp.zeros((R, A - 8), f32)], axis=1)
    full = jnp.concatenate([wide_found, jnp.zeros((3 * A - R, A), f32)], axis=0)
    flipped = [full[i * A : (i + 1) * A].T[0:8] for i in range(3)]
    fsend[0] = flipped[1]
    fsend[1] = flipped[2]

    def force_copy(g):
        return pltpu.make_async_remote_copy(
            src_ref=fsend.at[g // 2],
            dst_ref=frecv.at[g],
            send_sem=s4.at[g],
            recv_sem=r4.at[g],
            device_id=owners[g],
            device_id_type=MESH,
        )

    for g in (1, 3, 2, 0):
        force_copy(g).start()
    for g in range(4):
        force_copy(g).wait_recv()
    wide8 = lax.broadcasted_iota(jnp.int32, (8, A), 1)
    back_a = jnp.where(wide8 < GF, frecv[0], frecv[1])
    back_b = jnp.where(wide8 < GC, frecv[2], frecv[3])
    back = jnp.concatenate([back_a, back_b[:, 0 : 2 * GC]], axis=1)
    back = back + 0.0
    hi, lo = split(back)
    total = flipped[0] + dot(hi, pick) + dot(lo, pick)
    force_ref[...] = total[0:3] + total[3:6]

    sums = stage_end(2)
    energy_ref[...] = sums[0:1, 0:1] / sums[1:2, 0:1]

    for g in range(4):
        first_copy(g).wait_send()
        force_copy(g).wait_send()
        for part in range(len(CHUNKS)):
            moment_copy(g, part).wait_send()
            slope_copy(g, part).wait_send()
    for stage, (count, mine, where, buf, send, recv) in enumerate(stages):
        for s in range(1, count):
            stage_copy(stage, lax.rem(mine + s, count), mine).wait_send()


def on_device(
    sizes,
    features,
    positions,
    neighbours,
    neighbour_counts,
    domain_counts,
    face_lists,
    corner_lists,
    w_center,
    w_neigh,
    w_radial,
    w_latent,
    w_readout,
    w_energy,
):
    nx, ny = sizes
    inner = min(nx, 8)
    outer = nx // inner
    vmem = pltpu.VMEM
    dma = pltpu.SemaphoreType.DMA
    scratch = [
        vmem((2, GF + 8, C), f32),
        vmem((2, GC + 8, C), f32),
        vmem((2, GF + 8, C), f32),
        vmem((2, GC + 8, C), f32),
        vmem((3 * A, C), f32),
        vmem((C, 3 * A), bf16),
        vmem((C, A), f32),
        vmem((R + 4 * NB, PAIRS), bf16),
        vmem((R, PAIRS), bf16),
        vmem((K * NB, A), f32),
        vmem((9, K, A), f32),
        vmem((6 + NB, K, A), f32),
        vmem((C, PAIRS), f32),
        vmem((C, PAIRS), f32),
        vmem((C, PAIRS), f32),
        vmem((9 * C, PAIRS), bf16),
        vmem((A, 9 * C), f32),
        vmem((NG, 9 * C), f32),
        vmem((NG, 9 * C), f32),
        vmem((NG, 9 * C), f32),
        vmem((NG, 9 * C), f32),
        vmem((9 * C, R), bf16),
        vmem((C, PAIRS), f32),
        vmem((K * 16, A), f32),
        vmem((K * NB, A), f32),
        vmem((8, PAIRS), bf16),
        vmem((2, 8, A), f32),
        vmem((4, 8, A), f32),
        vmem((inner, 8, C), f32),
        vmem((outer, 8, C), f32),
        vmem((ny, 8, C), f32),
        dma((4,)),
        dma((4,)),
        dma((16,)),
        dma((16,)),
        dma((16,)),
        dma((16,)),
        dma((4,)),
        dma((4,)),
        dma((inner,)),
        dma((inner,)),
        dma((outer,)),
        dma((outer,)),
        dma((ny,)),
        dma((ny,)),
    ]
    energy, forces = pl.pallas_call(
        functools.partial(kernel, sizes),
        out_shape=(
            jax.ShapeDtypeStruct((1, 1), f32),
            jax.ShapeDtypeStruct((3, A), f32),
        ),
        in_specs=[pl.BlockSpec(memory_space=pltpu.VMEM)] * 13,
        out_specs=(
            pl.BlockSpec(memory_space=pltpu.VMEM),
            pl.BlockSpec(memory_space=pltpu.VMEM),
        ),
        scratch_shapes=scratch,
        compiler_params=pltpu.CompilerParams(
            collective_id=0, has_side_effects=True, vmem_limit_bytes=50 * 1024 * 1024
        ),
    )(
        features[0, 0],
        positions[0, 0],
        neighbours[0, 0],
        neighbour_counts[0],
        domain_counts,
        face_lists[0, 0],
        corner_lists[0, 0],
        w_center,
        w_neigh,
        w_radial,
        w_latent,
        w_readout,
        w_energy[None, :],
    )
    return (energy.reshape(()), forces[None, None])


def solution(mesh):
    sizes = (mesh.shape["gx"], mesh.shape["gy"])
    placed = (
        P("gx", "gy", None, None),
        P("gx", "gy", None, None),
        P("gx", "gy", None, None),
        P("gx", "gy", None),
        P("gx", "gy"),
        P("gx", "gy", None, None),
        P("gx", "gy", None, None),
        P(),
        P(),
        P(),
        P(),
        P(),
        P(),
    )
    return jax.shard_map(
        functools.partial(on_device, sizes),
        mesh=mesh,
        in_specs=placed,
        out_specs=(P(), P("gx", "gy", None, None)),
        check_vma=False,
    )
```

time: 501 us -> 79.4 us (0.16); the launches traced: 492 us -> 78.9 us
  local copies, waits for them, and re-layouts: 183 us -> 7.2 us
  other arithmetic: 135 us -> 0 us
  blocking collectives: 77.2 us -> 0 us
  Pallas kernels: 0 us -> 68.6 us
  starting transfers between devices: 44.3 us -> 0 us
  matrix products: 36 us -> 0 us
  waiting for transfers between devices: 11.5 us -> 0 us
    psum x1 -> x0, blocking collectives: 77.2 us -> none  [on_device(): lax.psum((local_total, live_count.astype(jnp.float32)), ('gx', 'gy'))]
    gather x19 -> x0, local copies, waits for them, and re-layouts: 76.2 us -> none  [the longest x8 47.1 us: add_block(): jax.ops.segment_sum(term, index_block, num_segments=total_rows)]
    scatter-add x7 -> x0, other arithmetic: 74.4 us -> none  [the longest x4 45.6 us: add_block(): jax.ops.segment_sum(term, index_block, num_segments=total_rows)]
    pallas_call x0 -> x1, Pallas kernels: none -> 68.6 us  [on_device(): pl.pallas_call(functools.partial(kernel, sizes), out_shape=(jax.ShapeDtyp...]
    ppermute x21 -> x0, starting transfers between devices: 44.3 us -> none  [from_behind(): return lax.ppermute(block, axis, route)]
    mul x20 -> x0, local copies, waits for them, and re-layouts: 40.1 us -> none  [the longest x16 36.6 us: add_block(): jnp.transpose(harm_block)[:, :, None] * weight_block[:, None, :]]
    dot_general x12 -> x0, matrix products: 36 us -> none  [the longest x3 20.2 us: pair_terms(): jnp.einsum('mka,kac->amc', harm, weight, precision=lax.Precision.HIGHEST)]
    dynamic_update_slice x24 -> x0, local copies, waits for them, and re-layouts: 22.3 us -> none  [pair_terms(): lax.scan(add_block, start, (signed, weight_blocks, index_blocks))]
  transfers between devices with their start and end apart: 21 -> 0, of which waited for: 7 -> 0; matrix products, arithmetic and copies ran while one was open for 12% -> 0% of each run, Pallas kernels for 0% -> 0%
where the time goes in v1:
time: 79.4 us; the launch traced here: 78.9 us
  Pallas kernels  68.6 us (86%)
  local copies, waits for them, and re-layouts  7.2 us (9%)
  between operations  3.08 us (4%)
    pallas_call x1, Pallas kernels, on_device(): pl.pallas_call(functools.partial(kernel, sizes), out_shape=(jax.ShapeDtyp...  68.6 us
    unnamed x24, local copies, waits for them, and re-layouts  7.2 us

profile of v1, /device:TPU:1, one launch (start us, length us, event | category | flops | bytes accessed | tf_op | source)
XLA Modules:
  0.0 78.9 jit_solution(1060080350329709357)
XLA Ops:
  0.6 0.0 copy-start.5
  1.3 0.0 copy-start.8
  1.3 0.7 copy.18
  2.0 0.0 copy-start.7
  2.0 0.0 copy-start.9
  2.0 0.0 copy-done.5
  2.0 0.0 copy-done.8
  2.0 0.7 copy-done.7
  2.7 0.0 copy-done.9
  2.7 0.0 copy-start
  2.7 0.9 %copy-done = bf16[384,128]{1,0:T(8,128)(2,1)S(1)} copy-done((bf16[384,128]{1,0:T(8,128)(2,1)S(1)}, bf16[384,128]{1,0:T(8,128)(2,1)}, u32[]{:S(2)}) %copy-start) | copy-done | bytes 98328
  3.6 0.0 copy-start.1
  3.6 0.8 copy-done.1
  4.3 0.0 copy-start.2
  4.3 0.8 copy-done.2
  5.1 0.0 copy-start.3
  5.1 0.8 copy-done.3
  5.8 0.0 copy-start.4
  5.9 0.8 copy-done.4
  6.6 0.0 copy-start.6
  6.6 0.7 copy-done.6
  7.3 0.0 copy-start.10
  7.3 0.7 copy-done.10
  8.0 68.6 %shard_map.140 = (f32[1,1]{1,0:T(1,128)}, f32[3,128]{1,0:T(4,128)S(1)}) custom-call(bf16[128,128]{1,0:T(8,128)(2,1)S(1)} %bitcast.11, f32[3,128]{1,0:T(4,128)S(1)} %bitcast.13, s32[32,128]{1,0:T(8,128)S(1)} %bitcast.12, s32[1,128]{1,0:T(1,128)S(1)} %bitcast.17, s32[1,1]{1,0:T(1,128)S(6)} %copy.20.dom_ref, s32[2,64]{1,0:T(2,128)S(1)} %bitcast.15, ...), custom_call_target="tpu_custom_call" | custom-call | tf_op jit(solution)/shard_map/pallas_call | solution.py:615
  76.5 0.6 copy.15
Async XLA Ops:
  0.6 1.4 %copy-start.5 = (s32[1,1,32,128]{3,2,1,0:T(8,128)S(1)}, s32[1,1,32,128]{3,2,1,0:T(8,128)}, u32[]{:S(2)}) copy-start(s32[1,1,32,128]{3,2,1,0:T(8,128)} %param.15) | copy-start | bytes 49156
  1.3 0.7 copy-start.8
  2.0 0.7 copy-start.7
  2.0 0.7 copy-start.9
  2.7 0.9 %copy-start = (bf16[384,128]{1,0:T(8,128)(2,1)S(1)}, bf16[384,128]{1,0:T(8,128)(2,1)}, u32[]{:S(2)}) copy-start(bf16[384,128]{1,0:T(8,128)(2,1)} %wo_ref.1) | copy-start | bytes 294916
  3.6 0.8 copy-start.1
  4.3 0.8 copy-start.2
  5.1 0.8 copy-start.3
  5.8 0.8 copy-start.4
  6.6 0.7 copy-start.6
  7.3 0.7 copy-start.10

commit v2 on v1

--- a/solution.py
+++ b/solution.py
@@ -27,7 +27,8 @@
 STEP = 4
 WIDE = STEP * A
 ORDER = (0, 4, 5, 6, 7, 8, 1, 2, 3)
-CHUNKS = ((0, 2), (2, 4), (4, 6), (6, 9))
+MOMENT_PARTS = ((0, 2), (2, 4), (4, 6), (6, 9))
+SLOPE_PARTS = ((6, 7), (7, 9), (4, 6), (2, 4), (1, 2), (0, 1))
 GROUPS = ((0, GF), (GF, GF), (2 * GF, GC), (2 * GF + GC, GC))
 
 
@@ -57,6 +58,21 @@
 
 def kernel(
     sizes,
+    feat_hbm,
+    pos_hbm,
+    nbr_hbm,
+    cnt_hbm,
+    dom_hbm,
+    face_hbm,
+    corner_hbm,
+    wc_hbm,
+    wn_hbm,
+    wr_hbm,
+    wl_hbm,
+    wo_hbm,
+    we_hbm,
+    energy_ref,
+    force_ref,
     feat_ref,
     pos_ref,
     nbr_ref,
@@ -70,8 +86,10 @@
     wl_ref,
     wo_ref,
     we_ref,
-    energy_ref,
-    force_ref,
+    load_sem,
+    force_out,
+    energy_out,
+    out_sem,
     outf,
     outc,
     inf,
@@ -82,21 +100,23 @@
     even,
     odd,
     brow,
+    drow,
+    slow,
     harm,
+    tiles,
     geom,
-    lat,
-    d1s,
-    d2s,
+    pres,
+    acts,
     term,
     mom,
+    halves,
     msend,
     mrecv,
     slope_send,
     slope_recv,
     gt,
-    dw,
-    dys,
-    dbs,
+    ays,
+    bys,
     ddr,
     fsend,
     frecv,
@@ -152,6 +172,32 @@
     for target in greeted:
         pl.semaphore_signal(barrier, inc=1, device_id=target, device_id_type=MESH)
 
+    first_loads = [
+        (face_hbm, face_ref),
+        (corner_hbm, corner_ref),
+        (feat_hbm, feat_ref),
+        (pos_hbm, pos_ref),
+    ]
+    later_loads = [
+        (nbr_hbm, nbr_ref),
+        (wn_hbm, wn_ref),
+        (wc_hbm, wc_ref),
+        (wr_hbm, wr_ref),
+        (cnt_hbm, cnt_ref),
+        (dom_hbm, dom_ref),
+        (wl_hbm, wl_ref),
+        (wo_hbm, wo_ref),
+        (we_hbm, we_ref),
+    ]
+    loads = [
+        pltpu.make_async_copy(src, dst, load_sem.at[i])
+        for i, (src, dst) in enumerate(first_loads + later_loads)
+    ]
+    for load in loads:
+        load.start()
+    for load in loads[: len(first_loads)]:
+        load.wait()
+
     sub = lax.broadcasted_iota(jnp.int32, (A, A), 0)
     lane = lax.broadcasted_iota(jnp.int32, (A, A), 1)
     eye = jnp.where(sub == lane, 1.0, 0.0)
@@ -166,7 +212,7 @@
     picked = dot(pick, feat)
     small = lax.broadcasted_iota(jnp.int32, (3, A), 0)
     wide = lax.broadcasted_iota(jnp.int32, (3, A), 1)
-    pos = pos_ref[...]
+    pos = jnp.concatenate([pos_ref[c] for c in range(3)], axis=0)
     zero = jnp.zeros((3, A), f32)
     at_a = pick_lanes(pos, jnp.broadcast_to(lists_a, (3, A)))
     at_b = pick_lanes(pos, jnp.broadcast_to(jnp.maximum(lists_b, 0), (3, A)))
@@ -181,19 +227,25 @@
 
     pl.semaphore_wait(barrier, len(greeted))
 
+    def wait_bytes(ref, sem):
+        pltpu.make_async_copy(ref, ref, sem).wait()
+
     def first_copy(g):
         src, dst, slot = (outf, inf, g) if g < 2 else (outc, inc, g - 2)
         return pltpu.make_async_remote_copy(
             src_ref=src.at[slot],
             dst_ref=dst.at[slot],
-            send_sem=s1.at[g],
-            recv_sem=r1.at[g],
+            send_sem=s1.at[g // 2],
+            recv_sem=r1.at[g // 2],
             device_id=holders[g],
             device_id_type=MESH,
         )
 
     for g in (1, 3, 2, 0):
         first_copy(g).start()
+
+    for load in loads[len(first_loads) :]:
+        load.wait()
 
     proj[0:A, :] = dot(feat, wn_ref[...])
     center = dot(feat, wc_ref[...])
@@ -222,8 +274,8 @@
 
     lax.fori_loop(0, K, build, 0)
 
-    for g in range(4):
-        first_copy(g).wait_recv()
+    wait_bytes(inf, r1.at[0])
+    wait_bytes(inc, r1.at[1])
     for g, (base, rows) in enumerate(GROUPS):
         buf, slot = (inf, g) if g < 2 else (inc, g - 2)
         proj[A + base : A + base + rows, :] = dot(
@@ -285,7 +337,9 @@
     for n in range(1, NB + 1):
         value = norm * s_now * inv
         brow[pl.ds(n - 1, K, stride=NB), :] = value
-        geom[5 + n] = norm * (n * math.pi / cutoff) * c_now * inv - value * inv
+        drow[pl.ds(n - 1, K, stride=NB), :] = (
+            norm * (n * math.pi / cutoff) * c_now * inv - value * inv
+        )
         s_old, s_now = s_now, 2.0 * cos1 * s_now - s_old
         c_old, c_now = c_now, 2.0 * cos1 * c_now - c_old
 
@@ -295,6 +349,13 @@
         hi = tile.astype(bf16).astype(f32)
         rows = jnp.concatenate([hi, tile - hi, hi, jnp.zeros_like(hi)], axis=0)
         even[R : R + 4 * NB, lanes] = rows.astype(bf16)
+        tile = drow[pl.ds(pl.multiple_of(k * NB, NB), NB), :]
+        hi = tile.astype(bf16).astype(f32)
+        rows = jnp.concatenate([hi, tile - hi, hi, jnp.zeros_like(hi)], axis=0)
+        slow[:, lanes] = rows.astype(bf16)
+        for at in range(1, 9):
+            row = jnp.broadcast_to(harm[at, pl.ds(k, 1), :], (16, A))
+            tiles[at, pl.ds(k, 1)] = row.astype(bf16)[None]
         return carry
 
     lax.fori_loop(0, K, put_basis, 0)
@@ -305,56 +366,86 @@
     def forward(q, carry):
         lanes = pl.ds(pl.multiple_of(q * WIDE, WIDE), WIDE)
         pre = dot(left[:, 0 : R + 4 * NB], even[:, lanes]) + cent_wide
-        hidden, d1 = silu_parts(pre)
-        d1s[:, lanes] = d1
-        latent, d2 = silu_parts(dot(wl_t, hidden.astype(bf16)))
-        lat[:, lanes] = latent
-        d2s[:, lanes] = d2
+        pres[:, lanes] = pre
+        hidden = pre * (0.5 + 0.5 * jnp.tanh(0.5 * pre))
+        act = dot(wl_t, hidden.astype(bf16))
+        acts[:, lanes] = act
+        latent = act * (0.5 + 0.5 * jnp.tanh(0.5 * act))
         for s in range(STEP):
             k = q * STEP + s
             cols = pl.ds(pl.multiple_of(k * A, A), A)
             w = latent[:, s * A : (s + 1) * A] * geom[0, pl.ds(k, 1), :]
-            for at, m in enumerate(ORDER):
-                value = w * harm[at, pl.ds(k, 1), :] if m else w
-                term[at * C : (at + 1) * C, cols] = value.astype(bf16)
+            term[0:C, cols] = w.astype(bf16)
         return carry
 
-    lax.fori_loop(0, K // STEP, forward, 0)
-
-    def group_copy(src, dst, send, recv, g, part, targets):
+    lax.fori_loop(0, K // STEP, forward, 0, unroll=8)
+
+    def group_copy(src, dst, send, recv, g, part, targets, parts):
         base, rows = GROUPS[g]
-        first, last = CHUNKS[part]
+        first, last = parts[part]
         view = (pl.ds(base, rows), pl.ds(first * C, (last - first) * C))
-        sem = part * 4 + g
         return pltpu.make_async_remote_copy(
             src_ref=src.at[view],
             dst_ref=dst.at[view],
-            send_sem=send.at[sem],
-            recv_sem=recv.at[sem],
+            send_sem=send.at[part],
+            recv_sem=recv.at[part],
             device_id=targets[g],
             device_id_type=MESH,
         )
 
+    def wait_part(ref, sem, parts, part):
+        first, last = parts[part]
+        wait_bytes(ref.at[:, pl.ds(first * C, (last - first) * C)], sem.at[part])
+
     def moment_copy(g, part):
-        return group_copy(msend, mrecv, s2, r2, g, part, owners)
+        return group_copy(msend, mrecv, s2, r2, g, part, owners, MOMENT_PARTS)
 
     def slope_copy(g, part):
-        return group_copy(slope_send, slope_recv, s3, r3, g, part, holders)
-
-    for part, (first, last) in enumerate(CHUNKS):
+        return group_copy(slope_send, slope_recv, s3, r3, g, part, holders, SLOPE_PARTS)
+
+    def build_terms(first, last):
+        for at in range(max(first, 1), last):
+            for k in range(K):
+                cols = slice(k * A, (k + 1) * A)
+                tile = jnp.concatenate([tiles[at, k]] * (C // 16), axis=0)
+                term[at * C : (at + 1) * C, cols] = term[0:C, cols] * tile
+
+    build_terms(*MOMENT_PARTS[0])
+    for part, (first, last) in enumerate(MOMENT_PARTS):
+        if part + 1 < len(MOMENT_PARTS):
+            build_terms(*MOMENT_PARTS[part + 1])
         cols = slice(first * C, last * C)
         side = even if first < 6 else odd
-        found = dot_nt(side[0:R, :], term[cols, :])
-        mom[:, cols] = found[0:A]
-        msend[:, cols] = found[A:R]
+        half = PAIRS // 2
+        size = (last - first) * C
+        halves[0, :, 0:size] = dot_nt(side[0:R, 0:half], term[cols, 0:half])
+        halves[1, :, 0:size] = dot_nt(side[0:R, half:], term[cols, half:])
+        mom[:, cols] = halves[0, 0:A, 0:size] + halves[1, 0:A, 0:size]
+        msend[:, cols] = halves[0, A:R, 0:size] + halves[1, A:R, 0:size]
         for g in (1, 3, 2, 0):
             moment_copy(g, part).start()
 
+    def slope_of_latents(q, carry):
+        lanes = pl.ds(pl.multiple_of(q * WIDE, WIDE), WIDE)
+        unused_hidden, d1 = silu_parts(pres[:, lanes])
+        d_hidden = d1 * dot(left[:, R : R + 4 * NB], slow[:, lanes])
+        latent, d2 = silu_parts(acts[:, lanes])
+        d_latent = d2 * dot(wl_t, d_hidden.astype(bf16))
+        for s in range(STEP):
+            k = q * STEP + s
+            cols = pl.ds(pl.multiple_of(k * A, A), A)
+            here = slice(s * A, (s + 1) * A)
+            env, d_env = geom[0, pl.ds(k, 1), :], geom[1, pl.ds(k, 1), :]
+            pres[:, cols] = latent[:, here] * env
+            acts[:, cols] = d_latent[:, here] * env + latent[:, here] * d_env
+        return carry
+
+    lax.fori_loop(0, K // STEP, slope_of_latents, 0, unroll=2)
+
     spread2 = jnp.concatenate([spread, spread], axis=1)
-    for part, (first, last) in enumerate(CHUNKS):
+    for part, (first, last) in enumerate(MOMENT_PARTS):
         cols = slice(first * C, last * C)
-        for g in range(4):
-            moment_copy(g, part).wait_recv()
+        wait_part(mrecv, r2, MOMENT_PARTS, part)
         hi, lo = split(mrecv[:, cols])
         mom[:, cols] = mom[:, cols] + dot(spread2, jnp.concatenate([hi, lo], axis=0))
 
@@ -376,23 +467,24 @@
     pick2 = jnp.concatenate([pick, pick], axis=1)
     scale = [2.0 * d_inv[:, i * C : (i + 1) * C] / (1.0 + sums[i]) for i in range(3)]
     which = (0, 2, 2, 2, 2, 2, 1, 1, 1)
-    for part, (first, last) in enumerate(CHUNKS):
+    for part, (first, last) in enumerate(SLOPE_PARTS):
         for at in range(first, last):
             cols = slice(at * C, (at + 1) * C)
             value = mom[:, cols] * scale[which[at]]
             hi, lo = split(value)
             slope_send[:, cols] = dot(pick2, jnp.concatenate([hi, lo], axis=0))
             gt[cols, 0:A] = value.T.astype(bf16)
-        for g in (1, 3, 2, 0):
-            slope_copy(g, part).start()
+        if part < 2:
+            for g in (1, 3, 2, 0):
+                slope_copy(g, part).start()
 
     def stage_copy(stage, peer, slot):
         count, mine, where, buf, send, recv = stages[stage]
         return pltpu.make_async_remote_copy(
             src_ref=buf.at[mine],
             dst_ref=buf.at[slot],
-            send_sem=send.at[peer],
-            recv_sem=recv.at[slot],
+            send_sem=send.at[0],
+            recv_sem=recv.at[0],
             device_id=where(peer),
             device_id_type=MESH,
         )
@@ -405,9 +497,8 @@
 
     def stage_end(stage):
         count, mine, where, buf, send, recv = stages[stage]
-        for s in range(1, count):
-            peer = lax.rem(mine + s, count)
-            stage_copy(stage, peer, peer).wait_recv()
+        if count > 1:
+            wait_bytes(buf.at[pl.ds(0, count - 1)], recv.at[0])
         total = buf[0]
         for i in range(1, count):
             total = total + buf[i]
@@ -417,75 +508,42 @@
     pair = jnp.where(half == 0, own_energy, dom_ref[...].astype(f32))
     stage_start(0, pair)
 
-    def pull(q, lo_row, hi_row):
+    def pull(part, q, carry):
+        first, last = SLOPE_PARTS[part]
+        side = even if first < 6 else odd
         lanes = pl.ds(pl.multiple_of(q * WIDE, WIDE), WIDE)
-        at_even = dot(gt[0 : 6 * C, lo_row:hi_row], even[lo_row:hi_row, lanes])
-        at_odd = dot(gt[6 * C : 9 * C, lo_row:hi_row], odd[lo_row:hi_row, lanes])
-        outs = []
+        found = dot(gt[first * C : last * C, :], side[0:R, lanes])
         for s in range(STEP):
             k = q * STEP + s
             cols = pl.ds(pl.multiple_of(k * A, A), A)
-            w = lat[:, cols] * geom[0, pl.ds(k, 1), :]
-            total = None
-            rows = []
-            for at, m in enumerate(ORDER):
-                part = at_even if at < 6 else at_odd
-                base = (at if at < 6 else at - 6) * C
-                h = part[base : base + C, s * A : (s + 1) * A]
-                if m:
-                    rows.append(jnp.sum(h * w, axis=0, keepdims=True))
-                    total = total + h * harm[at, pl.ds(k, 1), :]
-                else:
-                    total = h
-            outs.append((total, rows))
-        return outs
-
-    def pull_own(q, carry):
-        for s, (total, rows) in enumerate(pull(q, 0, A)):
-            k = q * STEP + s
-            dw[:, pl.ds(pl.multiple_of(k * A, A), A)] = total
-            for at, row in enumerate(rows):
-                dys[pl.ds(k * 16 + at, 1), :] = row
+            w, d_w = pres[:, cols], acts[:, cols]
+            for at in range(first, last):
+                base = (at - first) * C
+                h = found[base : base + C, s * A : (s + 1) * A]
+                spot = pl.ds(k * 16 + at, 1)
+                if at:
+                    ays[spot, :] = jnp.sum(h * w, axis=0, keepdims=True)
+                bys[spot, :] = jnp.sum(h * d_w, axis=0, keepdims=True)
         return carry
 
-    lax.fori_loop(0, K // STEP, pull_own, 0)
-    stage_start(1, stage_end(0))
-
-    for part, (first, last) in enumerate(CHUNKS):
-        for g in range(4):
-            slope_copy(g, part).wait_recv()
+    for part, (first, last) in enumerate(SLOPE_PARTS):
+        wait_part(slope_recv, r3, SLOPE_PARTS, part)
+        for later in ((2, 3), (4,), (5,), (), (), ())[part]:
+            for g in (1, 3, 2, 0):
+                slope_copy(g, later).start()
         for at in range(first, last):
             cols = slice(at * C, (at + 1) * C)
             gt[cols, A : 2 * A] = slope_recv[0:A, cols].T.astype(bf16)
             gt[cols, 2 * A : R] = slope_recv[A:NG, cols].T.astype(bf16)
-
-    wl = wl_ref[...]
-    wr2 = jnp.concatenate([wr_hi, wr - wr_hi], axis=0).astype(bf16)
-
-    def pull_ghost(q, carry):
-        for s, (total, rows) in enumerate(pull(q, A, R)):
-            k = q * STEP + s
-            cols = pl.ds(pl.multiple_of(k * A, A), A)
-            d_w = dw[:, cols] + total
-            for at, row in enumerate(rows):
-                spot = pl.ds(k * 16 + at, 1)
-                dys[spot, :] = dys[spot, :] + row
-            dys[pl.ds(k * 16 + 8, 1), :] = jnp.sum(d_w * lat[:, cols], axis=0, keepdims=True)
-            d_pre2 = d_w * geom[0, pl.ds(k, 1), :] * d2s[:, cols]
-            d_hidden = dot(wl, d_pre2.astype(bf16)).astype(bf16).astype(f32)
-            hi, lo = split(d_hidden * d1s[:, cols])
-            two = dot(wr2, hi)
-            d_basis = two[0:NB] + two[NB : 2 * NB] + dot(wr2[0:NB], lo)
-            dbs[pl.ds(pl.multiple_of(k * NB, NB), NB), :] = d_basis
-        return carry
-
-    lax.fori_loop(0, K // STEP, pull_ghost, 0)
+        lax.fori_loop(0, K // STEP, functools.partial(pull, part), 0, unroll=4)
+        if part == 2:
+            stage_start(1, stage_end(0))
     stage_start(2, stage_end(1))
 
-    g_of = {m: dys[pl.ds(at - 1, K, stride=16), :] for at, m in enumerate(ORDER) if m}
-    d_radius = dys[pl.ds(8, K, stride=16), :] * geom[1]
-    for n in range(1, NB + 1):
-        d_radius = d_radius + dbs[pl.ds(n - 1, K, stride=NB), :] * geom[5 + n]
+    g_of = {m: ays[pl.ds(at, K, stride=16), :] for at, m in enumerate(ORDER) if m}
+    d_radius = bys[pl.ds(0, K, stride=16), :]
+    for at in range(1, 9):
+        d_radius = d_radius + bys[pl.ds(at, K, stride=16), :] * harm[at]
     inv, ux, uy, uz = geom[2], geom[3], geom[4], geom[5]
     dux = root3 * g_of[1] + root15 * (uy * g_of[4] + uz * g_of[7] + ux * g_of[8])
     duy = root3 * g_of[2] + root15 * (ux * g_of[4] + uz * g_of[5] - uy * g_of[8])
@@ -511,16 +569,15 @@
         return pltpu.make_async_remote_copy(
             src_ref=fsend.at[g // 2],
             dst_ref=frecv.at[g],
-            send_sem=s4.at[g],
-            recv_sem=r4.at[g],
+            send_sem=s4.at[0],
+            recv_sem=r4.at[0],
             device_id=owners[g],
             device_id_type=MESH,
         )
 
     for g in (1, 3, 2, 0):
         force_copy(g).start()
-    for g in range(4):
-        force_copy(g).wait_recv()
+    wait_bytes(frecv, r4.at[0])
     wide8 = lax.broadcasted_iota(jnp.int32, (8, A), 1)
     back_a = jnp.where(wide8 < GF, frecv[0], frecv[1])
     back_b = jnp.where(wide8 < GC, frecv[2], frecv[3])
@@ -528,20 +585,29 @@
     back = back + 0.0
     hi, lo = split(back)
     total = flipped[0] + dot(hi, pick) + dot(lo, pick)
-    force_ref[...] = total[0:3] + total[3:6]
-
+    for c in range(3):
+        force_out[c] = -(total[c : c + 1] + total[c + 3 : c + 4])
     sums = stage_end(2)
-    energy_ref[...] = sums[0:1, 0:1] / sums[1:2, 0:1]
-
-    for g in range(4):
-        first_copy(g).wait_send()
-        force_copy(g).wait_send()
-        for part in range(len(CHUNKS)):
-            moment_copy(g, part).wait_send()
-            slope_copy(g, part).wait_send()
-    for stage, (count, mine, where, buf, send, recv) in enumerate(stages):
-        for s in range(1, count):
-            stage_copy(stage, lax.rem(mine + s, count), mine).wait_send()
+    energy_out[...] = sums[0:1, 0:1] / sums[1:2, 0:1]
+    outs = [
+        pltpu.make_async_copy(force_out, force_ref, out_sem.at[0]),
+        pltpu.make_async_copy(energy_out, energy_ref, out_sem.at[1]),
+    ]
+    for out in outs:
+        out.start()
+
+    for out in outs:
+        out.wait()
+    wait_bytes(outf, s1.at[0])
+    wait_bytes(outc, s1.at[1])
+    wait_bytes(frecv, s4.at[0])
+    for part in range(len(MOMENT_PARTS)):
+        wait_part(msend, s2, MOMENT_PARTS, part)
+    for part in range(len(SLOPE_PARTS)):
+        wait_part(slope_send, s3, SLOPE_PARTS, part)
+    for count, mine, where, buf, send, recv in stages:
+        if count > 1:
+            wait_bytes(buf.at[pl.ds(0, count - 1)], send.at[0])
 
 
 def on_device(
@@ -566,6 +632,23 @@
     vmem = pltpu.VMEM
     dma = pltpu.SemaphoreType.DMA
     scratch = [
+        vmem((A, C), bf16),
+        vmem((3, 1, A), f32),
+        vmem((K, A), jnp.int32),
+        vmem((1, A), jnp.int32),
+        vmem((1, 1), jnp.int32),
+        vmem((2, GF), jnp.int32),
+        vmem((2, GC), jnp.int32),
+        vmem((C, C), bf16),
+        vmem((C, C), bf16),
+        vmem((NB, C), f32),
+        vmem((C, C), bf16),
+        vmem((3 * C, C), bf16),
+        vmem((1, C), f32),
+        dma((13,)),
+        vmem((3, 1, A), f32),
+        vmem((1, 1), f32),
+        dma((2,)),
         vmem((2, GF + 8, C), f32),
         vmem((2, GC + 8, C), f32),
         vmem((2, GF + 8, C), f32),
@@ -576,60 +659,62 @@
         vmem((R + 4 * NB, PAIRS), bf16),
         vmem((R, PAIRS), bf16),
         vmem((K * NB, A), f32),
+        vmem((K * NB, A), f32),
+        vmem((4 * NB, PAIRS), bf16),
         vmem((9, K, A), f32),
-        vmem((6 + NB, K, A), f32),
-        vmem((C, PAIRS), f32),
+        vmem((9, K, 16, A), bf16),
+        vmem((6, K, A), f32),
         vmem((C, PAIRS), f32),
         vmem((C, PAIRS), f32),
         vmem((9 * C, PAIRS), bf16),
         vmem((A, 9 * C), f32),
+        vmem((2, R, 3 * C), f32),
         vmem((NG, 9 * C), f32),
         vmem((NG, 9 * C), f32),
         vmem((NG, 9 * C), f32),
         vmem((NG, 9 * C), f32),
         vmem((9 * C, R), bf16),
-        vmem((C, PAIRS), f32),
         vmem((K * 16, A), f32),
-        vmem((K * NB, A), f32),
+        vmem((K * 16, A), f32),
         vmem((8, PAIRS), bf16),
         vmem((2, 8, A), f32),
         vmem((4, 8, A), f32),
         vmem((inner, 8, C), f32),
         vmem((outer, 8, C), f32),
         vmem((ny, 8, C), f32),
-        dma((4,)),
-        dma((4,)),
-        dma((16,)),
-        dma((16,)),
-        dma((16,)),
-        dma((16,)),
-        dma((4,)),
-        dma((4,)),
-        dma((inner,)),
-        dma((inner,)),
-        dma((outer,)),
-        dma((outer,)),
-        dma((ny,)),
-        dma((ny,)),
+        dma((2,)),
+        dma((2,)),
+        dma((len(MOMENT_PARTS),)),
+        dma((len(MOMENT_PARTS),)),
+        dma((len(SLOPE_PARTS),)),
+        dma((len(SLOPE_PARTS),)),
+        dma((1,)),
+        dma((1,)),
+        dma((1,)),
+        dma((1,)),
+        dma((1,)),
+        dma((1,)),
+        dma((1,)),
+        dma((1,)),
     ]
     energy, forces = pl.pallas_call(
         functools.partial(kernel, sizes),
         out_shape=(
             jax.ShapeDtypeStruct((1, 1), f32),
-            jax.ShapeDtypeStruct((3, A), f32),
+            jax.ShapeDtypeStruct((3, 1, A), f32),
         ),
-        in_specs=[pl.BlockSpec(memory_space=pltpu.VMEM)] * 13,
+        in_specs=[pl.BlockSpec(memory_space=pltpu.HBM)] * 13,
         out_specs=(
-            pl.BlockSpec(memory_space=pltpu.VMEM),
-            pl.BlockSpec(memory_space=pltpu.VMEM),
+            pl.BlockSpec(memory_space=pl.ANY),
+            pl.BlockSpec(memory_space=pl.ANY),
         ),
         scratch_shapes=scratch,
         compiler_params=pltpu.CompilerParams(
-            collective_id=0, has_side_effects=True, vmem_limit_bytes=50 * 1024 * 1024
+            collective_id=0, has_side_effects=True, vmem_limit_bytes=61900 * 1024
         ),
     )(
         features[0, 0],
-        positions[0, 0],
+        jnp.transpose(positions, (0, 2, 1, 3))[0],
         neighbours[0, 0],
         neighbour_counts[0],
         domain_counts,
@@ -642,7 +727,7 @@
         w_readout,
         w_energy[None, :],
     )
-    return (energy.reshape(()), forces[None, None])
+    return (energy.reshape(()), -jnp.transpose(forces[None], (0, 2, 1, 3)))
 
 
 def solution(mesh):

time: 79.4 us -> 63.5 us (0.80)
  Pallas kernels: 68.6 us -> 59.1 us
  local copies, waits for them, and re-layouts: 7.2 us -> 0.65 us
    pallas_call x1, Pallas kernels: 68.6 us -> 59.1 us  [on_device(): pl.pallas_call(functools.partial(kernel, sizes), out_shape=(jax.ShapeDtyp...]
    unnamed x24 -> x2, local copies, waits for them, and re-layouts: 7.2 us -> 0.65 us
where the time goes in v2:
time: 63.5 us; the launch traced here: 63.4 us
  Pallas kernels  59.1 us (93%)
  between operations  3.06 us (5%)
  local copies, waits for them, and re-layouts  0.65 us (1%)
    pallas_call x1, Pallas kernels, on_device(): pl.pallas_call(functools.partial(kernel, sizes), out_shape=(jax.ShapeDtyp...  59.1 us

profile of v2, /device:TPU:1, one launch (start us, length us, event | category | flops | bytes accessed | tf_op | source)
XLA Modules:
  0.0 63.4 jit_solution(8767592903064332882)
XLA Ops:
  1.3 59.1 %shard_map.140 = (f32[1,1]{1,0:T(1,128)}, f32[3,1,128]{2,1,0:T(1,128)}) custom-call(bf16[128,128]{1,0:T(8,128)(2,1)} %bitcast.12, f32[3,1,128]{2,1,0:T(1,128)} %bitcast.14, s32[32,128]{1,0:T(8,128)} %bitcast.13, s32[1,128]{1,0:T(1,128)} %bitcast.17, s32[1,1]{1,0:T(1,128)S(6)} %copy.17.dom_hbm, s32[2,64]{1,0:T(2,128)} %bitcast.15, s32[2,16]{1,0:T(2,128)} %bitcast.16, ...), custom_call_target="tpu_custom_call" | custom-call | tf_op jit(solution)/shard_map/pallas_call | solution.py:700
  60.4 0.0 copy-start
  60.4 0.6 %copy-done = f32[3,1,128]{2,1,0:T(1,128)S(1)} copy-done((f32[3,1,128]{2,1,0:T(1,128)S(1)}, f32[3,1,128]{2,1,0:T(1,128)}, u32[]{:S(2)}) %copy-start) | copy-done | bytes 1560
  61.0 0.6 negate_bitcast_fusion
Async XLA Ops:
  60.4 0.7 %copy-start = (f32[3,1,128]{2,1,0:T(1,128)S(1)}, f32[3,1,128]{2,1,0:T(1,128)}, u32[]{:S(2)}) copy-start(f32[3,1,128]{2,1,0:T(1,128)} %get-tuple-element.5) | copy-start | bytes 4612

commit v3 on v2

--- a/solution.py
+++ b/solution.py
@@ -26,9 +26,11 @@
 PAIRS = K * A
 STEP = 4
 WIDE = STEP * A
+PULL_STEP = 4
+PULL_WIDE = PULL_STEP * A
 ORDER = (0, 4, 5, 6, 7, 8, 1, 2, 3)
 MOMENT_PARTS = ((0, 2), (2, 4), (4, 6), (6, 9))
-SLOPE_PARTS = ((6, 7), (7, 9), (4, 6), (2, 4), (1, 2), (0, 1))
+SLOPE_PARTS = ((6, 9), (4, 6), (2, 4), (0, 2))
 GROUPS = ((0, GF), (GF, GF), (2 * GF, GC), (2 * GF + GC, GC))
 
 
@@ -109,7 +111,6 @@
     acts,
     term,
     mom,
-    halves,
     msend,
     mrecv,
     slope_send,
@@ -416,12 +417,10 @@
             build_terms(*MOMENT_PARTS[part + 1])
         cols = slice(first * C, last * C)
         side = even if first < 6 else odd
-        half = PAIRS // 2
         size = (last - first) * C
-        halves[0, :, 0:size] = dot_nt(side[0:R, 0:half], term[cols, 0:half])
-        halves[1, :, 0:size] = dot_nt(side[0:R, half:], term[cols, half:])
-        mom[:, cols] = halves[0, 0:A, 0:size] + halves[1, 0:A, 0:size]
-        msend[:, cols] = halves[0, A:R, 0:size] + halves[1, A:R, 0:size]
+        found = dot_nt(side[0:R, :], term[cols, :])
+        mom[:, cols] = found[0:A]
+        msend[:, cols] = found[A:R]
         for g in (1, 3, 2, 0):
             moment_copy(g, part).start()
 
@@ -440,7 +439,7 @@
             acts[:, cols] = d_latent[:, here] * env + latent[:, here] * d_env
         return carry
 
-    lax.fori_loop(0, K // STEP, slope_of_latents, 0, unroll=2)
+    lax.fori_loop(0, K // STEP, slope_of_latents, 0, unroll=4)
 
     spread2 = jnp.concatenate([spread, spread], axis=1)
     for part, (first, last) in enumerate(MOMENT_PARTS):
@@ -511,10 +510,10 @@
     def pull(part, q, carry):
         first, last = SLOPE_PARTS[part]
         side = even if first < 6 else odd
-        lanes = pl.ds(pl.multiple_of(q * WIDE, WIDE), WIDE)
+        lanes = pl.ds(pl.multiple_of(q * PULL_WIDE, PULL_WIDE), PULL_WIDE)
         found = dot(gt[first * C : last * C, :], side[0:R, lanes])
-        for s in range(STEP):
-            k = q * STEP + s
+        for s in range(PULL_STEP):
+            k = q * PULL_STEP + s
             cols = pl.ds(pl.multiple_of(k * A, A), A)
             w, d_w = pres[:, cols], acts[:, cols]
             for at in range(first, last):
@@ -526,17 +525,21 @@
                 bys[spot, :] = jnp.sum(h * d_w, axis=0, keepdims=True)
         return carry
 
+    def pull_all(part):
+        step = functools.partial(pull, part)
+        lax.fori_loop(0, K // PULL_STEP, step, 0, unroll=8)
+
     for part, (first, last) in enumerate(SLOPE_PARTS):
         wait_part(slope_recv, r3, SLOPE_PARTS, part)
-        for later in ((2, 3), (4,), (5,), (), (), ())[part]:
+        for later in ((2,), (3,), (), ())[part]:
             for g in (1, 3, 2, 0):
                 slope_copy(g, later).start()
         for at in range(first, last):
             cols = slice(at * C, (at + 1) * C)
             gt[cols, A : 2 * A] = slope_recv[0:A, cols].T.astype(bf16)
             gt[cols, 2 * A : R] = slope_recv[A:NG, cols].T.astype(bf16)
-        lax.fori_loop(0, K // STEP, functools.partial(pull, part), 0, unroll=4)
-        if part == 2:
+        pull_all(part)
+        if part == 1:
             stage_start(1, stage_end(0))
     stage_start(2, stage_end(1))
 
@@ -668,7 +671,6 @@
         vmem((C, PAIRS), f32),
         vmem((9 * C, PAIRS), bf16),
         vmem((A, 9 * C), f32),
-        vmem((2, R, 3 * C), f32),
         vmem((NG, 9 * C), f32),
         vmem((NG, 9 * C), f32),
         vmem((NG, 9 * C), f32),

time: 63.5 us -> 61 us (0.961)
  Pallas kernels: 59.1 us -> 56.6 us
    pallas_call x1, Pallas kernels: 59.1 us -> 56.6 us  [on_device(): pl.pallas_call(functools.partial(kernel, sizes), out_shape=(jax.ShapeDtyp...]
where the time goes in v3:
time: 61 us; the launch traced here: 60.9 us
  Pallas kernels  56.6 us (93%)
  between operations  3.06 us (5%)
  local copies, waits for them, and re-layouts  0.65 us (1%)
    pallas_call x1, Pallas kernels, on_device(): pl.pallas_call(functools.partial(kernel, sizes), out_shape=(jax.ShapeDtyp...  56.6 us

profile of v3, /device:TPU:1, one launch (start us, length us, event | category | flops | bytes accessed | tf_op | source)
XLA Modules:
  0.0 60.9 jit_solution(2927997701535322385)
XLA Ops:
  1.3 56.6 %shard_map.140 = (f32[1,1]{1,0:T(1,128)}, f32[3,1,128]{2,1,0:T(1,128)}) custom-call(bf16[128,128]{1,0:T(8,128)(2,1)} %bitcast.12, f32[3,1,128]{2,1,0:T(1,128)} %bitcast.14, s32[32,128]{1,0:T(8,128)} %bitcast.13, s32[1,128]{1,0:T(1,128)} %bitcast.17, s32[1,1]{1,0:T(1,128)S(6)} %copy.17.dom_hbm, s32[2,64]{1,0:T(2,128)} %bitcast.15, s32[2,16]{1,0:T(2,128)} %bitcast.16, ...), custom_call_target="tpu_custom_call" | custom-call | tf_op jit(solution)/shard_map/pallas_call | solution.py:702
  57.9 0.0 copy-start
  57.9 0.6 %copy-done = f32[3,1,128]{2,1,0:T(1,128)S(1)} copy-done((f32[3,1,128]{2,1,0:T(1,128)S(1)}, f32[3,1,128]{2,1,0:T(1,128)}, u32[]{:S(2)}) %copy-start) | copy-done | bytes 1560
  58.5 0.6 negate_bitcast_fusion
Async XLA Ops:
  57.9 0.7 %copy-start = (f32[3,1,128]{2,1,0:T(1,128)S(1)}, f32[3,1,128]{2,1,0:T(1,128)}, u32[]{:S(2)}) copy-start(f32[3,1,128]{2,1,0:T(1,128)} %get-tuple-element.5) | copy-start | bytes 4612

commit v4 on v3

--- a/solution.py
+++ b/solution.py
@@ -381,28 +381,26 @@
 
     lax.fori_loop(0, K // STEP, forward, 0, unroll=8)
 
-    def group_copy(src, dst, send, recv, g, part, targets, parts):
+    def group_copy(src, dst, send, recv, g, part, targets):
         base, rows = GROUPS[g]
-        first, last = parts[part]
-        view = (pl.ds(base, rows), pl.ds(first * C, (last - first) * C))
+        view = pl.ds(base, rows)
         return pltpu.make_async_remote_copy(
-            src_ref=src.at[view],
-            dst_ref=dst.at[view],
+            src_ref=src[part].at[view],
+            dst_ref=dst[part].at[view],
             send_sem=send.at[part],
             recv_sem=recv.at[part],
             device_id=targets[g],
             device_id_type=MESH,
         )
 
-    def wait_part(ref, sem, parts, part):
-        first, last = parts[part]
-        wait_bytes(ref.at[:, pl.ds(first * C, (last - first) * C)], sem.at[part])
+    def wait_part(refs, sem, part):
+        wait_bytes(refs[part], sem.at[part])
 
     def moment_copy(g, part):
-        return group_copy(msend, mrecv, s2, r2, g, part, owners, MOMENT_PARTS)
+        return group_copy(msend, mrecv, s2, r2, g, part, owners)
 
     def slope_copy(g, part):
-        return group_copy(slope_send, slope_recv, s3, r3, g, part, holders, SLOPE_PARTS)
+        return group_copy(slope_send, slope_recv, s3, r3, g, part, holders)
 
     def build_terms(first, last):
         for at in range(max(first, 1), last):
@@ -420,7 +418,7 @@
         size = (last - first) * C
         found = dot_nt(side[0:R, :], term[cols, :])
         mom[:, cols] = found[0:A]
-        msend[:, cols] = found[A:R]
+        msend[part][...] = found[A:R]
         for g in (1, 3, 2, 0):
             moment_copy(g, part).start()
 
@@ -444,8 +442,8 @@
     spread2 = jnp.concatenate([spread, spread], axis=1)
     for part, (first, last) in enumerate(MOMENT_PARTS):
         cols = slice(first * C, last * C)
-        wait_part(mrecv, r2, MOMENT_PARTS, part)
-        hi, lo = split(mrecv[:, cols])
+        wait_part(mrecv, r2, part)
+        hi, lo = split(mrecv[part][...])
         mom[:, cols] = mom[:, cols] + dot(spread2, jnp.concatenate([hi, lo], axis=0))
 
     levels = ((0, 1), (6, 9), (1, 6))
@@ -471,7 +469,8 @@
             cols = slice(at * C, (at + 1) * C)
             value = mom[:, cols] * scale[which[at]]
             hi, lo = split(value)
-            slope_send[:, cols] = dot(pick2, jnp.concatenate([hi, lo], axis=0))
+            there = slice((at - first) * C, (at - first + 1) * C)
+            slope_send[part][:, there] = dot(pick2, jnp.concatenate([hi, lo], axis=0))
             gt[cols, 0:A] = value.T.astype(bf16)
         if part < 2:
             for g in (1, 3, 2, 0):
@@ -530,14 +529,15 @@
         lax.fori_loop(0, K // PULL_STEP, step, 0, unroll=8)
 
     for part, (first, last) in enumerate(SLOPE_PARTS):
-        wait_part(slope_recv, r3, SLOPE_PARTS, part)
+        wait_part(slope_recv, r3, part)
         for later in ((2,), (3,), (), ())[part]:
             for g in (1, 3, 2, 0):
                 slope_copy(g, later).start()
         for at in range(first, last):
             cols = slice(at * C, (at + 1) * C)
-            gt[cols, A : 2 * A] = slope_recv[0:A, cols].T.astype(bf16)
-            gt[cols, 2 * A : R] = slope_recv[A:NG, cols].T.astype(bf16)
+            there = slice((at - first) * C, (at - first + 1) * C)
+            gt[cols, A : 2 * A] = slope_recv[part][0:A, there].T.astype(bf16)
+            gt[cols, 2 * A : R] = slope_recv[part][A:NG, there].T.astype(bf16)
         pull_all(part)
         if part == 1:
             stage_start(1, stage_end(0))
@@ -605,9 +605,9 @@
     wait_bytes(outc, s1.at[1])
     wait_bytes(frecv, s4.at[0])
     for part in range(len(MOMENT_PARTS)):
-        wait_part(msend, s2, MOMENT_PARTS, part)
+        wait_part(msend, s2, part)
     for part in range(len(SLOPE_PARTS)):
-        wait_part(slope_send, s3, SLOPE_PARTS, part)
+        wait_part(slope_send, s3, part)
     for count, mine, where, buf, send, recv in stages:
         if count > 1:
             wait_bytes(buf.at[pl.ds(0, count - 1)], send.at[0])
@@ -634,6 +634,10 @@
     outer = nx // inner
     vmem = pltpu.VMEM
     dma = pltpu.SemaphoreType.DMA
+
+    def held(parts):
+        return tuple(vmem((NG, (last - first) * C), f32) for first, last in parts)
+
     scratch = [
         vmem((A, C), bf16),
         vmem((3, 1, A), f32),
@@ -671,10 +675,10 @@
         vmem((C, PAIRS), f32),
         vmem((9 * C, PAIRS), bf16),
         vmem((A, 9 * C), f32),
-        vmem((NG, 9 * C), f32),
-        vmem((NG, 9 * C), f32),
-        vmem((NG, 9 * C), f32),
-        vmem((NG, 9 * C), f32),
+        held(MOMENT_PARTS),
+        held(MOMENT_PARTS),
+        held(SLOPE_PARTS),
+        held(SLOPE_PARTS),
         vmem((9 * C, R), bf16),
         vmem((K * 16, A), f32),
         vmem((K * 16, A), f32),

time: 61 us -> 61 us (level)
  no operation moved by 1% of the time
where the time goes in v4:
time: 61 us; the launch traced here: 60.9 us
  Pallas kernels  56.6 us (93%)
  between operations  3.06 us (5%)
  local copies, waits for them, and re-layouts  0.65 us (1%)
    pallas_call x1, Pallas kernels, on_device(): pl.pallas_call(functools.partial(kernel, sizes), out_shape=(jax.ShapeDtyp...  56.6 us

profile of v4, /device:TPU:1, one launch (start us, length us, event | category | flops | bytes accessed | tf_op | source)
XLA Modules:
  0.0 60.9 jit_solution(15284589309158637866)
XLA Ops:
  1.3 56.6 %shard_map.140 = (f32[1,1]{1,0:T(1,128)}, f32[3,1,128]{2,1,0:T(1,128)}) custom-call(bf16[128,128]{1,0:T(8,128)(2,1)} %bitcast.12, f32[3,1,128]{2,1,0:T(1,128)} %bitcast.14, s32[32,128]{1,0:T(8,128)} %bitcast.13, s32[1,128]{1,0:T(1,128)} %bitcast.17, s32[1,1]{1,0:T(1,128)S(6)} %copy.17.dom_hbm, s32[2,64]{1,0:T(2,128)} %bitcast.15, s32[2,16]{1,0:T(2,128)} %bitcast.16, ...), custom_call_target="tpu_custom_call" | custom-call | tf_op jit(solution)/shard_map/pallas_call | solution.py:706
  57.9 0.0 copy-start
  57.9 0.6 %copy-done = f32[3,1,128]{2,1,0:T(1,128)S(1)} copy-done((f32[3,1,128]{2,1,0:T(1,128)S(1)}, f32[3,1,128]{2,1,0:T(1,128)}, u32[]{:S(2)}) %copy-start) | copy-done | bytes 1560
  58.5 0.6 negate_bitcast_fusion
Async XLA Ops:
  57.9 0.7 %copy-start = (f32[3,1,128]{2,1,0:T(1,128)S(1)}, f32[3,1,128]{2,1,0:T(1,128)}, u32[]{:S(2)}) copy-start(f32[3,1,128]{2,1,0:T(1,128)} %get-tuple-element.5) | copy-start | bytes 4612
